TPU v7x, 32 devices: a whole 2x2x4 slice. The times are simulated.
32 devices in a mesh: seq: 16 (over z, y, core), head: 2 (over x).
Axes of the slice: x: 2, y: 2, z: 4, core: 2. Of those that a mesh axis runs over, the one named last changes fastest.
Arguments:
- queries: bfloat16 [6144, 768], P('seq', 'head'), as said below
- keys: bfloat16 [6144, 768], P('seq', 'head'), as said below
- values: bfloat16 [6144, 768], P('seq', 'head'), may hold values from -6 to 6
- image_tiles: int32 [5], replicated, may hold values from 1 to 21, 48 in all
Outputs:
- attended: bfloat16 [6144, 768], P(('seq', 'head'))
Inputs may be any that keep to these rules, and one draw needn't show every extreme that they name: `image_tiles`: the 5 images fill all 48 tiles in order; the longest holds exactly 21 tiles. `queries`: entries lie within -6 and 6. `keys`: entries lie within -6 and 6.
All inputs are finite; a program needn't handle non-finite values.
Results may differ from a plain program's by a relative error of at most 0.007.
Values may be sent and summed in bfloat16 or wider, within the bound.
No kernel may reach another device: no remote copies, remote signals or barrier semaphores. Data moves between devices by JAX's collectives and lax.ppermute only.
A program may use at most 64 MiB of HBM per device.

v0:
```python
import functools
import math

import jax
import jax.numpy as jnp
from jax import lax
from jax.experimental import pallas as pl
from jax.experimental.pallas import tpu as pltpu
from jax.sharding import PartitionSpec as P

HEAD_DIM = 128
TILE = 128
MOST_TILES = 21

LOWEST = -1e30
SCALE2 = math.log2(math.e) / math.sqrt(HEAD_DIM)
COST = 1

VMEM = pl.BlockSpec(memory_space=pltpu.VMEM)
SMEM = pl.BlockSpec(memory_space=pltpu.SMEM)
HBM = pl.BlockSpec(memory_space=pl.ANY)


def params():
    return pltpu.CompilerParams(vmem_limit_bytes=16 * 1024 * 1024)


def head_columns(h):
    return slice(h * HEAD_DIM, (h + 1) * HEAD_DIM)


def tile_rows(t):
    return slice(t * TILE, (t + 1) * TILE)


def image_bounds(tiles_ref, tile):
    first = jnp.int32(0)
    start, end = jnp.int32(0), jnp.int32(0)
    for i in range(tiles_ref.shape[0]):
        after = first + tiles_ref[i]
        inside = (tile >= first) & (tile < after)
        start = jnp.where(inside, first, start)
        end = jnp.where(inside, after, end)
        first = after
    return start, end


def meta_kernel(halves, tiles_ref, bounds_ref, far_ref):
    tiles = bounds_ref.shape[1] // TILE
    me = lax.axis_index("seq")
    bounds_ref[...] = jnp.zeros(bounds_ref.shape, jnp.int32)
    for half, owner in enumerate(halves(me)):
        for t in range(tiles):
            start, end = image_bounds(tiles_ref, owner * tiles + t)
            bounds_ref[2 * half : 2 * half + 1, tile_rows(t)] = jnp.full((1, TILE), start, jnp.int32)
            bounds_ref[2 * half + 1 : 2 * half + 2, tile_rows(t)] = jnp.full((1, TILE), end, jnp.int32)
    first = jnp.int32(0)
    far = jnp.int32(0)
    for i in range(tiles_ref.shape[0]):
        after = first + tiles_ref[i]
        levels = (after - 1) // (4 * tiles) - first // (4 * tiles)
        far = jnp.where(levels >= 2, 1, far)
        first = after
    far_ref[0] = far
    bounds_ref[8:9] = jnp.full((1, bounds_ref.shape[1]), far, jnp.int32)


def meta(halves, image_tiles, rows):
    bounds, far = pl.pallas_call(
        functools.partial(meta_kernel, halves),
        out_shape=[jax.ShapeDtypeStruct((16, rows), jnp.int32), jax.ShapeDtypeStruct((1,), jnp.int32)],
        in_specs=[SMEM],
        out_specs=[VMEM, SMEM],
        compiler_params=params(),
        cost_estimate=pl.CostEstimate(flops=COST * 2**28, bytes_accessed=0, transcendentals=0),
        name="meta",
    )(image_tiles)
    return bounds, far[0]


def pack_kernel(k_ref, v_ref, out_ref, held, sems):
    rows, columns = k_ref.shape
    tiles = rows // TILE
    copies = []
    for t in range(tiles):
        copies.append(pltpu.make_async_copy(v_ref.at[tile_rows(t)], held.at[tile_rows(t)], sems.at[2 * t]))
        copies.append(pltpu.make_async_copy(k_ref.at[tile_rows(t)], out_ref.at[tile_rows(2 * t)], sems.at[2 * t + 1]))
    for copy in copies:
        copy.start()
    for t in range(tiles):
        copies[2 * t].wait()
        for h in range(columns // HEAD_DIM):
            out_ref[tile_rows(2 * t + 1), head_columns(h)] = held[tile_rows(t), head_columns(h)].T
    for copy in copies[1::2]:
        copy.wait()


def pack(keys, values):
    rows, columns = keys.shape
    return pl.pallas_call(
        pack_kernel,
        out_shape=jax.ShapeDtypeStruct((2 * rows, columns), keys.dtype),
        in_specs=[HBM, HBM],
        out_specs=VMEM,
        scratch_shapes=[pltpu.VMEM(values.shape, values.dtype), pltpu.SemaphoreType.DMA((2 * rows // TILE,))],
        name="pack",
    )(keys, values)


def onward_kernel(a1_ref, b1_ref, own_ref, near_ref, corner_ref):
    upper = lax.axis_index("seq") % 2
    rows = corner_ref.shape[0]

    @pl.when(upper == 0)
    def _():
        near_ref[...] = a1_ref[...]
        corner_ref[...] = b1_ref[:rows]

    @pl.when(upper == 1)
    def _():
        near_ref[...] = b1_ref[...]
        corner_ref[...] = a1_ref[-rows:]


def onward(a1, b1, own):
    rows, columns = a1.shape
    return pl.pallas_call(
        onward_kernel,
        out_shape=[
            jax.ShapeDtypeStruct((rows, columns), a1.dtype),
            jax.ShapeDtypeStruct((rows - 2 * TILE, columns), a1.dtype),
        ],
        in_specs=[VMEM, VMEM, HBM],
        out_specs=[VMEM, VMEM],
        compiler_params=params(),
        name="onward",
    )(a1, b1, own)


def summands(rows):
    parts = []
    for _ in range(3):
        parts.append(rows.astype(jnp.bfloat16))
        rows = rows - parts[-1].astype(jnp.float32)
    return parts


def attend_kernel(which, places, arrays, fresh, unless_far, brief, bounds_ref, *refs):
    halves = len(which)
    q_refs, refs = refs[:halves], refs[halves:]
    array_refs, refs = refs[: len(arrays)], refs[len(arrays) :]
    old_refs, refs = (None, refs) if fresh else (refs[:halves], refs[halves:])
    new_refs, (held_q, held, state) = refs[:halves], refs[halves:]
    rows, columns = q_refs[0].shape
    tiles = rows // TILE
    count = held.shape[1] // 2 // TILE
    heads = columns // HEAD_DIM
    me = lax.axis_index("seq")

    for half in range(halves):
        held_q[half] = q_refs[half][...]
        if fresh:
            state[half, :columns] = jnp.zeros((columns, rows), jnp.float32)
            state[half, columns : columns + heads] = jnp.full((heads, rows), LOWEST, jnp.float32)
            state[half, columns + heads :] = jnp.zeros((state.shape[1] - columns - heads, rows), jnp.float32)
        else:
            state[half] = old_refs[half][...]
    for slot, (array, shift) in enumerate(arrays):
        size = array_refs[array].shape[0]
        if size < held.shape[1]:
            held[slot] = jnp.zeros(held.shape[1:], held.dtype)
        at = 0 if shift is None else pl.multiple_of(shift(me), 2 * TILE)
        held[slot, pl.ds(at, size)] = array_refs[array][...]
    begins = [bounds_ref[2 * w, 0] for w in which]
    stops = [bounds_ref[2 * w + 1, rows - 1] for w in which]

    far = bounds_ref[8, 0] if unless_far else None

    def chosen(at, options):
        return functools.reduce(lambda x, i: jnp.where(at == i, options[i], x), range(1, len(options)), options[0])

    def fold(half, slot, first):
        row = 2 * (which[0] + half * (which[-1] - which[0]) // max(len(which) - 1, 1))
        low = bounds_ref[pl.ds(row, 1), :]
        high = bounds_ref[pl.ds(row + 1, 1), :]
        off = [
            jnp.where((first + j >= low) & (first + j < high), 0.0, -LOWEST).astype(jnp.float32)
            for j in range(count)
        ]
        maxima = [[state[half, pl.ds(columns + h, 1), tile_rows(t)] for t in range(tiles)] for h in range(heads)]
        totals = [state[half, pl.ds(columns + heads + h, 1), :] for h in range(heads)]
        scores = [
            lax.dot_general(
                jnp.concatenate([held[slot, tile_rows(2 * j), head_columns(h)] for j in range(count)], axis=0),
                held_q[half, :, head_columns(h)],
                (((1,), (1,)), ((), ())),
                preferred_element_type=jnp.float32,
            )
            for h in range(heads)
        ]
        factors, sums, updates, largest = [], [], [], []
        for h in range(heads):
            factor, rounded, total, new = [], [], [], []
            for t in range(tiles):
                lanes = tile_rows(t)
                parts = [scores[h][tile_rows(j), lanes] for j in range(count)]
                new_max = maxima[h][t]
                for j in range(count):
                    new_max = jnp.maximum(new_max, jnp.max(parts[j], axis=0, keepdims=True) - off[j][:, lanes])
                scaled = new_max * SCALE2
                weights = [jnp.exp2(parts[j] * SCALE2 - (scaled + off[j][:, lanes])) for j in range(count)]
                factor.append(jnp.exp2((maxima[h][t] - new_max) * SCALE2))
                total.append(jnp.sum(functools.reduce(jnp.add, weights), axis=0, keepdims=True))
                new.append(new_max)
                rounded.append(jnp.concatenate([w.astype(jnp.bfloat16) for w in weights], axis=0))
            updates.append(
                jnp.dot(
                    jnp.concatenate([held[slot, tile_rows(2 * j + 1), head_columns(h)] for j in range(count)], axis=1),
                    jnp.concatenate(rounded, axis=1),
                    preferred_element_type=jnp.float32,
                )
            )
            factors.append(jnp.concatenate(factor, axis=1))
            sums.append(jnp.concatenate(total, axis=1))
            largest.append(jnp.concatenate(new, axis=1))
        for h in range(heads):
            own = head_columns(h)
            state[half, own] = state[half, own] * factors[h] + updates[h]
            state[half, pl.ds(columns + h, 1), :] = largest[h]
            state[half, pl.ds(columns + heads + h, 1), :] = totals[h] * factors[h] + sums[h]

    @pl.loop(0, halves * len(places))
    def _(unit):
        half, slot = unit // len(places), unit % len(places)
        first = chosen(slot, [place(me) for place in places])

        if unless_far:
            first = jnp.where(far > 0, -count, first)

        @pl.when((first < chosen(half, stops)) & (first + count > chosen(half, begins)))
        def _():
            fold(half, slot, first)

    for half in range(halves):
        if brief:
            new_refs[half][:columns] = state[half, :columns].astype(jnp.bfloat16)
            statistics = state[half, columns:]
            for n, part in enumerate(summands(statistics)):
                at = columns + n * 2 * 8
                new_refs[half][at : at + 2 * 8] = jnp.concatenate([part, part], axis=0)
        else:
            new_refs[half][...] = state[half]


def attend(bounds, queries, blocks, places, states, which=None, shifts=None, unless_far=False, brief=False):
    which = list(range(len(queries))) if which is None else which
    queries, states = [queries[w] for w in which], [states[w] for w in which] if states else []
    halves = len(which)
    rows, columns = queries[0].shape
    depth = blocks[0].shape[0]
    heads = columns // HEAD_DIM
    shape = jax.ShapeDtypeStruct((columns + -(-2 * heads // 8) * 8, rows), jnp.float32)
    arrays = list(enumerate(shifts or [None] * len(blocks)))
    pairs = halves * (rows // TILE) * heads * len(blocks) * (depth // 2 // TILE)
    sent = jax.ShapeDtypeStruct((columns + 3 * 2 * 8, rows), jnp.bfloat16)
    return pl.pallas_call(
        functools.partial(attend_kernel, which, places, arrays, not states, unless_far, brief),
        out_shape=[sent if brief else shape] * halves,
        in_specs=[VMEM] * (1 + halves + len(blocks) + len(states)),
        out_specs=[VMEM] * halves,
        scratch_shapes=[
            pltpu.VMEM((halves, rows, columns), queries[0].dtype),
            pltpu.VMEM((len(blocks), depth, columns), blocks[0].dtype),
            pltpu.VMEM((halves,) + shape.shape, jnp.float32),
        ],
        compiler_params=params(),
        cost_estimate=pl.CostEstimate(
            flops=COST * pairs * 4 * TILE * TILE * HEAD_DIM,
            bytes_accessed=2 * len(blocks) * depth * columns + 4 * halves * rows * columns,
            transcendentals=pairs * TILE * TILE,
        ),
        name="attend",
    )(bounds, *queries, *blocks, *states)


def merged(states, columns):
    heads = columns // HEAD_DIM
    for h in range(heads):
        maxima = [ref[columns + h : columns + h + 1] for ref in states]
        totals = [ref[columns + heads + h : columns + heads + h + 1] for ref in states]
        largest = functools.reduce(jnp.maximum, maxima)
        factors = [jnp.exp2((m - largest) * SCALE2) for m in maxima]
        total = functools.reduce(jnp.add, [f * t for f, t in zip(factors, totals)])
        parts = [ref[head_columns(h)] * (f / total) for ref, f in zip(states, factors)]
        yield head_columns(h), functools.reduce(jnp.add, parts).T


def finish_kernel(*refs):
    out_ref = refs[-1]
    for own, done in merged(refs[:-1], out_ref.shape[1]):
        out_ref[:, own] = done.astype(out_ref.dtype)


def finish(states, rows, columns):
    return pl.pallas_call(
        finish_kernel,
        out_shape=jax.ShapeDtypeStruct((rows, columns), jnp.bfloat16),
        in_specs=[VMEM] * len(states),
        out_specs=VMEM,
        compiler_params=params(),
        name="finish",
    )(*states)


def message_kernel(*refs):
    states, outs, held = refs[:4], refs[4:8], refs[8]
    rows = outs[0].shape[0] - 2 * 8
    columns = outs[0].shape[1]
    heads = columns // HEAD_DIM
    mine = lax.axis_index("head")
    for part in range(2):
        pair, (keep_ref, send_ref) = states[2 * part : 2 * part + 2], outs[2 * part : 2 * part + 2]
        logs = []
        rest = pair[1][columns:].astype(jnp.float32)
        statistics = functools.reduce(jnp.add, [rest[n * 2 * 8 : n * 2 * 8 + 8] for n in range(3)])
        for h in range(heads):
            maxima = [pair[0][columns + h : columns + h + 1], statistics[h : h + 1]]
            totals = [pair[0][columns + heads + h : columns + heads + h + 1], statistics[heads + h : heads + h + 1]]
            largest = jnp.maximum(*maxima)
            factors = [jnp.exp2((m - largest) * SCALE2) for m in maxima]
            total = factors[0] * totals[0] + factors[1] * totals[1]
            some = jnp.where(total > 0, total, 1.0)
            scale = [f / some for f in factors]
            own = head_columns(h)
            sums = pair[0][own] * scale[0] + pair[1][own].astype(jnp.float32) * scale[1]
            held[:, own] = sums.T.astype(held.dtype)
            log = jnp.where(total > 0, largest * SCALE2 + jnp.log2(some), LOWEST)
            logs += [part.astype(jnp.float32) for part in summands(log)]
        logs = jnp.concatenate(logs + [jnp.zeros((2 * 8 - len(logs), held.shape[0]), jnp.float32)], axis=0)
        later = pltpu.roll(logs, rows, 1)
        for ref, which in ((send_ref, 1 - mine), (keep_ref, mine)):
            ref[:rows] = held[pl.ds(pl.multiple_of(which * rows, 2 * 8), rows), :]
            ref[rows:] = jnp.where(which == 0, logs, later).astype(ref.dtype)


def messages(mine, peers):
    rows, columns = mine[0].shape[1], mine[0].shape[0] // HEAD_DIM * HEAD_DIM
    shape = jax.ShapeDtypeStruct((rows // 2 + 2 * 8, columns), jnp.bfloat16)
    return pl.pallas_call(
        message_kernel,
        out_shape=[shape] * 4,
        in_specs=[VMEM] * 4,
        out_specs=[VMEM] * 4,
        scratch_shapes=[pltpu.VMEM((rows, columns), jnp.bfloat16)],
        compiler_params=params(),
        name="message",
    )(*mine, *peers)


def settle_kernel(*refs):
    parts, out_ref, logs = refs[:4], refs[4], refs[5]
    rows, columns = out_ref.shape[0], parts[0].shape[1]
    heads = columns // HEAD_DIM
    mine = lax.axis_index("head")
    logs[...] = jnp.zeros(logs.shape, jnp.float32)
    for i, ref in enumerate(parts):
        summands = ref[rows:].astype(jnp.float32)
        for h in range(heads):
            at = i * heads + h
            logs[at : at + 1] = functools.reduce(jnp.add, [summands[3 * h + n : 3 * h + n + 1] for n in range(3)])
    turned = logs[...].T[:rows]
    for side, base in ((0, 1 - mine), (1, mine)):
        for h in range(heads):
            both = [turned[:, at : at + 1] for at in (2 * side * heads + h, (2 * side + 1) * heads + h)]
            largest = jnp.maximum(*both)
            weights = [jnp.exp2(x - largest) for x in both]
            sums = [ref[:rows, head_columns(h)].astype(jnp.float32) for ref in parts[2 * side : 2 * side + 2]]
            total = weights[0] + weights[1]
            done = sums[0] * (weights[0] / total) + sums[1] * (weights[1] / total)
            at = pl.multiple_of(base * columns + h * HEAD_DIM, HEAD_DIM)
            out_ref[:, pl.ds(at, HEAD_DIM)] = done.astype(out_ref.dtype)


def settle(diagonal, beside, across, own):
    rows, columns = own.shape[0] - 2 * 8, own.shape[1]
    return pl.pallas_call(
        settle_kernel,
        out_shape=jax.ShapeDtypeStruct((rows, 2 * columns), own.dtype),
        in_specs=[VMEM] * 4,
        out_specs=VMEM,
        scratch_shapes=[pltpu.VMEM((TILE, columns), jnp.float32)],
        compiler_params=params(),
        name="settle",
    )(diagonal, beside, across, own)


def chip_pairs(mesh):
    places = [tuple(getattr(d, "coords", ())) for d in mesh.devices[:, 0]]
    count = len(places)
    if count % 4 or not places[0] or mesh.shape["head"] != 2:
        return False
    cores = all(places[i] == places[i + 1] for i in range(0, count, 2))
    level = all(places[i][2] == places[i + 3][2] for i in range(0, count, 4))
    climb = all(places[i][2] != places[i + 4][2] for i in range(0, count - 4))
    return cores and level and climb


def paired_shards(owner_count, queries, keys, values, image_tiles):
    rows, columns = queries.shape
    tiles = rows // TILE
    owners = range(owner_count)

    def flip(s):
        return 1 - 2 * ((s // 2) % 2)

    def core(s):
        return s % 2

    def moved(array, source, takes=lambda s: True):
        pairs = [(source(s), s) for s in owners if takes(s) and 0 <= source(s) < owner_count]
        return lax.ppermute(array, "seq", pairs)

    across = lambda s: s + 2 * flip(s)
    near_side = lambda s: s + 4 * flip(s)
    far_side = lambda s: s - 4 * flip(s)
    along = lambda s: s + 4 * flip(s) * (1 - 2 * core(s))
    against = lambda s: s - 4 * flip(s) * (1 - 2 * core(s))
    sibling = lambda s: s + 1 - 2 * core(s)
    inner = lambda s: core(s) == (1 - (s // 2) % 2)

    OWN = lambda s: s * tiles
    A1 = lambda s: along(s) * tiles
    B1 = lambda s: against(s) * tiles
    A2 = lambda s: (s + 8 * flip(s)) * tiles
    B2 = lambda s: jnp.where(inner(s), s - 8 * flip(s), -owner_count) * tiles

    peers = moved(queries, across)
    block = pack(keys, values)
    a1, b1 = moved(block, along), moved(block, against)
    level = (queries, moved(queries, sibling), peers, moved(peers, sibling))
    bounds, far = meta(lambda s: [s, sibling(s), across(s), sibling(across(s))], image_tiles, rows)
    fold = functools.partial(attend, bounds, level)
    states = fold([block], [OWN], [], which=[0, 1]) + fold([block], [OWN], [], which=[2, 3])
    states = fold([b1], [B1], states, unless_far=True)

    def merge(blocks, places, states, shifts=None):
        beside, diagonal = fold(blocks, places, states, which=[1, 3], shifts=shifts, brief=True)
        beside, diagonal = moved(beside, sibling), moved(diagonal, sibling)
        mine, peer = fold(blocks, places, states, which=[0, 2], shifts=shifts)
        keep, over_x, over_y, over_both = messages([mine, beside], [peer, diagonal])
        pairs = [(2 * across(s) + 1 - x, 2 * s + x) for s in owners for x in range(2)]
        over_both = lax.ppermute(over_both, ("seq", "head"), pairs)
        over_y = moved(over_y, across)
        over_x = lax.ppermute(over_x, "head", [(0, 1), (1, 0)])
        return settle(over_both, over_x, over_y, keep)

    def near_only(block, a1, b1, states):
        return merge([a1], [A1], states)

    def both_ways(block, a1, b1, states):
        near, corner = onward(a1, b1, block)
        a2, b2 = moved(near, near_side), moved(corner, far_side, inner)
        states = fold([a1, b1], [A1, B1], states)
        return merge([a2, b2], [A2, B2], states, [None, lambda s: 2 * TILE * core(s)])

    return lax.cond(far > 0, both_ways, near_only, block, a1, b1, states)


def ring_shards(owner_count, queries, keys, values, image_tiles):
    rows, columns = queries.shape
    tiles = rows // TILE
    reach = min(owner_count - 1, -(-(MOST_TILES - 1) // tiles))
    block = pack(keys, values)
    bounds, _ = meta(lambda s: [s], image_tiles, rows)
    fold = functools.partial(attend, bounds, (queries,))
    up = [(i, i + 1) for i in range(owner_count - 1)]
    down = [(i + 1, i) for i in range(owner_count - 1)]
    below = above = block
    states = []
    held, places = [block], [lambda s: s * tiles]
    for k in range(1, reach + 1):
        below = lax.ppermute(below, "seq", up)
        above = lax.ppermute(above, "seq", down)
        states = fold(held, places, states)
        held, places = [below, above], [lambda s, k=k: (s - k) * tiles, lambda s, k=k: (s + k) * tiles]
    attended = finish(fold(held, places, states), rows, columns)
    return lax.all_to_all(attended, "head", split_axis=0, concat_axis=1, tiled=True)


def solution(mesh):
    owner_count = mesh.shape["seq"]
    plan = paired_shards if chip_pairs(mesh) else ring_shards
    placed = (P("seq", "head"), P("seq", "head"), P("seq", "head"), P())
    return jax.shard_map(
        functools.partial(plan, owner_count),
        mesh=mesh,
        in_specs=placed,
        out_specs=P(("seq", "head"), None),
        check_vma=False,
    )
```

profile of v0, /device:TPU:0, one launch (start us, length us, event | category | flops | bytes accessed | tf_op | source)
XLA Modules:
  0.0 56.4 jit_solution(8123385611289649329)
XLA Ops:
  0.0 0.0 copy-start.1
  0.0 0.0 copy-start
  0.0 3.0 %collective-permute-start.12 = (bf16[384,384]{1,0:T(8,128)(2,1)}, bf16[384,384]{1,0:T(8,128)(2,1)S(1)}, u32[]{:S(2)}, u32[]{:S(2)}) collective-permute-start(bf16[384,384]{1,0:T(8,128)(2,1)} %refs_0_.3), channel_id=1, source_target_pairs={{4,0},{6,2},{0,4},{2,6},{12,8},{14,10},{8,12},{10,14},{20,16},{22,... | collective-permute-start | bytes 884744 | tf_op jit(solution)/shard_map/ppermute | solution.py:421
  3.0 1.2 %pack.1.refs_2_ = bf16[768,384]{1,0:T(8,128)(2,1)S(1)} custom-call(bf16[384,384]{1,0:T(8,128)(2,1)} %k_ref.1, bf16[384,384]{1,0:T(8,128)(2,1)} %v_ref.1), custom_call_target="tpu_custom_call" | custom-call | tf_op jit(solution)/shard_map/pack/pallas_call | solution.py:100
  4.2 3.5 %collective-permute-start.16 = (bf16[768,384]{1,0:T(8,128)(2,1)S(1)}, bf16[768,384]{1,0:T(8,128)(2,1)S(1)}, u32[]{:S(2)}, u32[]{:S(2)}) collective-permute-start(bf16[768,384]{1,0:T(8,128)(2,1)S(1)} %pack.1.refs_2_), channel_id=1, source_target_pairs={{10,2},{12,4},{0,8},{18,10},{20,12},{6,14},{8,16},{26,18},{28,20},... | collective-permute-start | bytes 1769480 | tf_op jit(solution)/shard_map/ppermute | solution.py:421
  7.7 1.3 %collective-permute-start.13 = (bf16[768,384]{1,0:T(8,128)(2,1)S(1)}, bf16[768,384]{1,0:T(8,128)(2,1)S(1)}, u32[]{:S(2)}, u32[]{:S(2)}) collective-permute-start(bf16[768,384]{1,0:T(8,128)(2,1)S(1)} %pack.1.refs_2_), channel_id=1, source_target_pairs={{8,0},{14,6},{16,8},{2,10},{4,12},{22,14},{24,16},{10,18},{12,20},... | collective-permute-start | bytes 1769480 | tf_op jit(solution)/shard_map/ppermute | solution.py:421
  9.0 0.0 copy-done.1
  9.0 0.1 collective-permute-start.14
  9.2 1.1 %collective-permute-done.12.refs_0_.refs_2_ = bf16[384,384]{1,0:T(8,128)(2,1)S(1)} collective-permute-done((bf16[384,384]{1,0:T(8,128)(2,1)}, bf16[384,384]{1,0:T(8,128)(2,1)S(1)}, u32[]{:S(2)}, u32[]{:S(2)}) %collective-permute-start.12) | collective-permute-done | bytes 294944 | tf_op jit(solution)/shard_map/ppermute | solution.py:421
  10.3 0.0 collective-permute-start.15
  10.3 0.0 copy-done
  10.3 1.2 %meta.1 = (s32[16,384]{1,0:T(8,128)S(1)}, s32[1]{0:T(128)}) custom-call(s32[5]{0:T(128)S(1)} %copy-done), custom_call_target="tpu_custom_call" | custom-call | flops 268435456 | tf_op jit(solution)/shard_map/meta/pallas_call | solution.py:69
  12.1 0.0 collective-permute-done.14.refs_1_
  12.1 2.0 %attend.13 = (f32[392,384]{1,0:T(8,128)S(1)}, f32[392,384]{1,0:T(8,128)S(1)}) custom-call(s32[16,384]{1,0:T(8,128)S(1)} %get-tuple-element.107.bounds_ref, bf16[384,384]{1,0:T(8,128)(2,1)S(1)} %copy-done.1, bf16[384,384]{1,0:T(8,128)(2,1)S(1)} %collective-permute-done.14.refs_1_, bf16[768,384]{1,0:T(8,128)(2,1)S(1)} %pack.1.refs_2_), custom_call_target="tpu_custom_call" | custom-call | flops 452984832 | bytes 1769472 | tf_op jit(solution)/shard_map/attend/pallas_call | solution.py:266
  14.2 0.0 collective-permute-done.15.refs_1_.refs_3_
  14.2 0.3 attend.14
  14.5 6.3 %collective-permute-done.16.refs_4_ = bf16[768,384]{1,0:T(8,128)(2,1)S(1)} collective-permute-done((bf16[768,384]{1,0:T(8,128)(2,1)S(1)}, bf16[768,384]{1,0:T(8,128)(2,1)S(1)}, u32[]{:S(2)}, u32[]{:S(2)}) %collective-permute-start.16) | collective-permute-done | bytes 589856 | tf_op jit(solution)/shard_map/ppermute | solution.py:421
  20.8 0.6 %attend.15 = (f32[392,384]{1,0:T(8,128)S(1)}, f32[392,384]{1,0:T(8,128)S(1)}, f32[392,384]{1,0:T(8,128)S(1)}, f32[392,384]{1,0:T(8,128)S(1)}) custom-call(s32[16,384]{1,0:T(8,128)S(1)} %get-tuple-element.107.bounds_ref, bf16[384,384]{1,0:T(8,128)(2,1)S(1)} %copy-done.1, bf16[384,384]{1,0:T(8,128)(2,1)S(1)} %collective-permute-done.14.refs_1_, ...), custom_call_target="tpu_custom_call" | custom-call | flops 905969664 | bytes 2949120 | tf_op jit(solution)/shard_map/attend/pallas_call | solution.py:266
  21.4 0.0 collective-permute-done.13
  21.4 34.3 %conditional.1 = (bf16[192,768]{1,0:T(8,128)(2,1)S(1)}) conditional(s32[]{:T(128)} %bitcast, (s32[16,384]{1,0:T(8,128)S(1)}, bf16[384,384]{1,0:T(8,128)(2,1)S(1)}, bf16[384,384]{1,0:T(8,128)(2,1)S(1)}, bf16[768,384]{1,0:T(8,128)(2,1)S(1)}, f32[392,384]{1,0:T(8,128)S(1)}, /*index=5*/f32[392,384]{1,0:T(8,128)S(1)}, bf16[384,384]{1,0:T(8,128)(2,1)S(1)}, ...), branch_computations={%region_0.0_spmd, %region_1.0_spmd} | conditional | flops 3623878656 | bytes 16761120 | solution.py:466
  21.4 0.1 onward.1
  21.5 1.3 %collective-permute-start.5 = (bf16[768,384]{1,0:T(8,128)(2,1)S(1)}, bf16[768,384]{1,0:T(8,128)(2,1)S(1)}, u32[]{:S(2)}, u32[]{:S(2)}) collective-permute-start(bf16[768,384]{1,0:T(8,128)(2,1)S(1)} %get-tuple-element.76), channel_id=1, source_target_pairs={{8,0},{10,2},{16,8},{18,10},{4,12},{6,14},{24,16},{26,18},{12,20},... | collective-permute-start | bytes 1769480 | tf_op jit(solution)/shard_map/cond/branch_1_fun/ppermute | solution.py:421
  22.8 0.9 %collective-permute-start.6 = (bf16[512,384]{1,0:T(8,128)(2,1)S(1)}, bf16[512,384]{1,0:T(8,128)(2,1)S(1)}, u32[]{:S(2)}, u32[]{:S(2)}) collective-permute-start(bf16[512,384]{1,0:T(8,128)(2,1)S(1)} %get-tuple-element.77), channel_id=1, source_target_pairs={{12,4},{2,10},{20,12},{10,18},{28,20},{18,26},{13,5},{3,11},{21,13... | collective-permute-start | bytes 1179656 | tf_op jit(solution)/shard_map/cond/branch_1_fun/ppermute | solution.py:421
  23.7 3.3 %attend.10 = (f32[392,384]{1,0:T(8,128)S(1)}, f32[392,384]{1,0:T(8,128)S(1)}, f32[392,384]{1,0:T(8,128)S(1)}, f32[392,384]{1,0:T(8,128)S(1)}) custom-call(s32[16,384]{1,0:T(8,128)S(1)} %get-tuple-element.70.bounds_ref, bf16[384,384]{1,0:T(8,128)(2,1)S(1)} %get-tuple-element.71.refs_0_, bf16[384,384]{1,0:T(8,128)(2,1)S(1)} %get-tuple-element.78.refs_1_.refs_0_, ...), custom_call_target="tpu_custom_call" | custom-call | flops 1811939328 | bytes 3538944 | tf_op jit(solution)/shard_map/cond/branch_1_fun/attend/pallas_call | solution.py:266
  27.1 0.0 collective-permute-done.6.refs_3_
  27.1 12.1 %collective-permute-done.5.refs_2_ = bf16[768,384]{1,0:T(8,128)(2,1)S(1)} collective-permute-done((bf16[768,384]{1,0:T(8,128)(2,1)S(1)}, bf16[768,384]{1,0:T(8,128)(2,1)S(1)}, u32[]{:S(2)}, u32[]{:S(2)}) %collective-permute-start.5) | collective-permute-done | bytes 589856 | tf_op jit(solution)/shard_map/cond/branch_1_fun/ppermute | solution.py:421
  39.2 2.2 %attend.12 = (bf16[432,384]{1,0:T(8,128)(2,1)S(1)}, bf16[432,384]{1,0:T(8,128)(2,1)S(1)}) custom-call(s32[16,384]{1,0:T(8,128)S(1)} %get-tuple-element.70.bounds_ref, bf16[384,384]{1,0:T(8,128)(2,1)S(1)} %get-tuple-element.78.refs_1_.refs_0_, bf16[384,384]{1,0:T(8,128)(2,1)S(1)} %get-tuple-element.79.refs_3_.refs_1_, ...), custom_call_target="tpu_custom_call" | custom-call | flops 905969664 | bytes 2359296 | tf_op jit(solution)/shard_map/cond/branch_1_fun/attend/pallas_call | solution.py:266
  41.3 0.1 collective-permute-start.7
  41.4 0.5 collective-permute-start.8
  41.9 1.3 %attend.11 = (f32[392,384]{1,0:T(8,128)S(1)}, f32[392,384]{1,0:T(8,128)S(1)}) custom-call(s32[16,384]{1,0:T(8,128)S(1)} %get-tuple-element.70.bounds_ref, bf16[384,384]{1,0:T(8,128)(2,1)S(1)} %get-tuple-element.71.refs_0_, bf16[384,384]{1,0:T(8,128)(2,1)S(1)} %get-tuple-element.72.refs_2_.refs_1_, bf16[768,384]{1,0:T(8,128)(2,1)S(1)} %collective-permute-done.5.refs_2_, ...), custom_call_target="tpu_custom_call" | custom-call | flops 905969664 | bytes 2359296 | tf_op jit(solution)/shard_map/cond/branch_1_fun/attend/pallas_call | solution.py:266
  43.3 0.0 collective-permute-done.7.refs_1_
  43.3 0.3 collective-permute-done.8.refs_3_
  43.5 0.6 message.3
  44.1 0.1 collective-permute-start.9
  44.2 1.6 %collective-permute-start.10 = (bf16[208,384]{1,0:T(8,128)(2,1)S(1)}, bf16[208,384]{1,0:T(8,128)(2,1)S(1)}, u32[]{:S(2)}, u32[]{:S(2)}) collective-permute-start(bf16[208,384]{1,0:T(8,128)(2,1)S(1)} %get-tuple-element.93), channel_id=1, source_target_pairs={{0,1},{1,0},{2,3},{3,2},{4,5},{5,4},{6,7},{7,6},{8,9},{9,8},{10,11... | collective-permute-start | bytes 479240 | tf_op jit(solution)/shard_map/cond/branch_1_fun/ppermute | solution.py:454
  45.7 1.9 %collective-permute-start.11 = (bf16[208,384]{1,0:T(8,128)(2,1)S(1)}, bf16[208,384]{1,0:T(8,128)(2,1)S(1)}, u32[]{:S(2)}, u32[]{:S(2)}) collective-permute-start(bf16[208,384]{1,0:T(8,128)(2,1)S(1)} %get-tuple-element.94), channel_id=1, source_target_pairs={{4,0},{6,2},{0,4},{2,6},{12,8},{14,10},{8,12},{10,14},{20,16},{22,... | collective-permute-start | bytes 479240 | tf_op jit(solution)/shard_map/cond/branch_1_fun/ppermute | solution.py:421
  47.6 4.4 %collective-permute-done.9.refs_0_ = bf16[208,384]{1,0:T(8,128)(2,1)S(1)} collective-permute-done((bf16[208,384]{1,0:T(8,128)(2,1)S(1)}, bf16[208,384]{1,0:T(8,128)(2,1)S(1)}, u32[]{:S(2)}, u32[]{:S(2)}) %collective-permute-start.9) | collective-permute-done | bytes 159776 | tf_op jit(solution)/shard_map/cond/branch_1_fun/ppermute | solution.py:452
  52.0 1.4 %collective-permute-done.10.refs_1_ = bf16[208,384]{1,0:T(8,128)(2,1)S(1)} collective-permute-done((bf16[208,384]{1,0:T(8,128)(2,1)S(1)}, bf16[208,384]{1,0:T(8,128)(2,1)S(1)}, u32[]{:S(2)}, u32[]{:S(2)}) %collective-permute-start.10) | collective-permute-done | bytes 159776 | tf_op jit(solution)/shard_map/cond/branch_1_fun/ppermute | solution.py:454
  53.5 1.2 %collective-permute-done.11.refs_2_ = bf16[208,384]{1,0:T(8,128)(2,1)S(1)} collective-permute-done((bf16[208,384]{1,0:T(8,128)(2,1)S(1)}, bf16[208,384]{1,0:T(8,128)(2,1)S(1)}, u32[]{:S(2)}, u32[]{:S(2)}) %collective-permute-start.11) | collective-permute-done | bytes 159776 | tf_op jit(solution)/shard_map/cond/branch_1_fun/ppermute | solution.py:421
  54.6 0.8 %settle.3 = bf16[192,768]{1,0:T(8,128)(2,1)S(1)} custom-call(bf16[208,384]{1,0:T(8,128)(2,1)S(1)} %collective-permute-done.9.refs_0_, bf16[208,384]{1,0:T(8,128)(2,1)S(1)} %collective-permute-done.10.refs_1_, bf16[208,384]{1,0:T(8,128)(2,1)S(1)} %collective-permute-done.11.refs_2_, bf16[208,384]{1,0:T(8,128)(2,1)S(1)} %get-tuple-element.95.refs_3_), custom_call_target="tpu_custom_call" | custom-call | tf_op jit(solution)/shard_map/cond/branch_1_fun/settle/pallas_call | solution.py:386
  55.7 0.0 copy-start.2
  55.7 0.7 %copy-done.2 = bf16[192,768]{1,0:T(8,128)(2,1)} copy-done((bf16[192,768]{1,0:T(8,128)(2,1)}, bf16[192,768]{1,0:T(8,128)(2,1)S(1)}, u32[]{:S(2)}) %copy-start.2) | copy-done | bytes 294936
Async XLA Ops:
  0.0 9.0 %copy-start.1 = (bf16[384,384]{1,0:T(8,128)(2,1)S(1)}, bf16[384,384]{1,0:T(8,128)(2,1)}, u32[]{:S(2)}) copy-start(bf16[384,384]{1,0:T(8,128)(2,1)} %refs_0_.3) | copy-start | bytes 884740
  0.0 10.3 %copy-start = (s32[5]{0:T(128)S(1)}, s32[5]{0:T(128)}, u32[]{:S(2)}) copy-start(s32[5]{0:T(128)} %tiles_ref.1) | copy-start | bytes 64
  0.0 10.3 %collective-permute-start.12 = (bf16[384,384]{1,0:T(8,128)(2,1)}, bf16[384,384]{1,0:T(8,128)(2,1)S(1)}, u32[]{:S(2)}, u32[]{:S(2)}) collective-permute-start(bf16[384,384]{1,0:T(8,128)(2,1)} %refs_0_.3), channel_id=1, source_target_pairs={{4,0},{6,2},{0,4},{2,6},{12,8},{14,10},{8,12},{10,14},{20,16},{22,... | collective-permute-start | bytes 884744 | tf_op jit(solution)/shard_map/ppermute | solution.py:421
  4.2 16.6 %collective-permute-start.16 = (bf16[768,384]{1,0:T(8,128)(2,1)S(1)}, bf16[768,384]{1,0:T(8,128)(2,1)S(1)}, u32[]{:S(2)}, u32[]{:S(2)}) collective-permute-start(bf16[768,384]{1,0:T(8,128)(2,1)S(1)} %pack.1.refs_2_), channel_id=1, source_target_pairs={{10,2},{12,4},{0,8},{18,10},{20,12},{6,14},{8,16},{26,18},{28,20},... | collective-permute-start | bytes 1769480 | tf_op jit(solution)/shard_map/ppermute | solution.py:421
  7.7 13.7 %collective-permute-start.13 = (bf16[768,384]{1,0:T(8,128)(2,1)S(1)}, bf16[768,384]{1,0:T(8,128)(2,1)S(1)}, u32[]{:S(2)}, u32[]{:S(2)}) collective-permute-start(bf16[768,384]{1,0:T(8,128)(2,1)S(1)} %pack.1.refs_2_), channel_id=1, source_target_pairs={{8,0},{14,6},{16,8},{2,10},{4,12},{22,14},{24,16},{10,18},{12,20},... | collective-permute-start | bytes 1769480 | tf_op jit(solution)/shard_map/ppermute | solution.py:421
  9.0 3.1 %collective-permute-start.14 = (bf16[384,384]{1,0:T(8,128)(2,1)S(1)}, bf16[384,384]{1,0:T(8,128)(2,1)S(1)}, u32[]{:S(2)}, u32[]{:S(2)}) collective-permute-start(bf16[384,384]{1,0:T(8,128)(2,1)S(1)} %copy-done.1), channel_id=1, source_target_pairs={{2,0},{0,2},{6,4},{4,6},{10,8},{8,10},{14,12},{12,14},{18,16},{16,... | collective-permute-start | bytes 884744 | tf_op jit(solution)/shard_map/ppermute | solution.py:421
  10.3 3.9 %collective-permute-start.15 = (bf16[384,384]{1,0:T(8,128)(2,1)S(1)}, bf16[384,384]{1,0:T(8,128)(2,1)S(1)}, u32[]{:S(2)}, u32[]{:S(2)}) collective-permute-start(bf16[384,384]{1,0:T(8,128)(2,1)S(1)} %collective-permute-done.12.refs_0_.refs_2_), channel_id=1, source_target_pairs={{2,0},{0,2},{6,4},{4,6},{10,8},{8,10},{14,12},{12,14},{18,16},{16,... | collective-permute-start | bytes 884744 | tf_op jit(solution)/shard_map/ppermute | solution.py:421
  21.5 17.6 %collective-permute-start.5 = (bf16[768,384]{1,0:T(8,128)(2,1)S(1)}, bf16[768,384]{1,0:T(8,128)(2,1)S(1)}, u32[]{:S(2)}, u32[]{:S(2)}) collective-permute-start(bf16[768,384]{1,0:T(8,128)(2,1)S(1)} %get-tuple-element.76), channel_id=1, source_target_pairs={{8,0},{10,2},{16,8},{18,10},{4,12},{6,14},{24,16},{26,18},{12,20},... | collective-permute-start | bytes 1769480 | tf_op jit(solution)/shard_map/cond/branch_1_fun/ppermute | solution.py:421
  22.8 4.2 %collective-permute-start.6 = (bf16[512,384]{1,0:T(8,128)(2,1)S(1)}, bf16[512,384]{1,0:T(8,128)(2,1)S(1)}, u32[]{:S(2)}, u32[]{:S(2)}) collective-permute-start(bf16[512,384]{1,0:T(8,128)(2,1)S(1)} %get-tuple-element.77), channel_id=1, source_target_pairs={{12,4},{2,10},{20,12},{10,18},{28,20},{18,26},{13,5},{3,11},{21,13... | collective-permute-start | bytes 1179656 | tf_op jit(solution)/shard_map/cond/branch_1_fun/ppermute | solution.py:421
  41.3 1.9 %collective-permute-start.7 = (bf16[432,384]{1,0:T(8,128)(2,1)S(1)}, bf16[432,384]{1,0:T(8,128)(2,1)S(1)}, u32[]{:S(2)}, u32[]{:S(2)}) collective-permute-start(bf16[432,384]{1,0:T(8,128)(2,1)S(1)} %get-tuple-element.89), channel_id=1, source_target_pairs={{2,0},{0,2},{6,4},{4,6},{10,8},{8,10},{14,12},{12,14},{18,16},{16,... | collective-permute-start | bytes 995336 | tf_op jit(solution)/shard_map/cond/branch_1_fun/ppermute | solution.py:421
  41.4 2.1 %collective-permute-start.8 = (bf16[432,384]{1,0:T(8,128)(2,1)S(1)}, bf16[432,384]{1,0:T(8,128)(2,1)S(1)}, u32[]{:S(2)}, u32[]{:S(2)}) collective-permute-start(bf16[432,384]{1,0:T(8,128)(2,1)S(1)} %get-tuple-element.91), channel_id=1, source_target_pairs={{2,0},{0,2},{6,4},{4,6},{10,8},{8,10},{14,12},{12,14},{18,16},{16,... | collective-permute-start | bytes 995336 | tf_op jit(solution)/shard_map/cond/branch_1_fun/ppermute | solution.py:421
  44.1 8.0 %collective-permute-start.9 = (bf16[208,384]{1,0:T(8,128)(2,1)S(1)}, bf16[208,384]{1,0:T(8,128)(2,1)S(1)}, u32[]{:S(2)}, u32[]{:S(2)}) collective-permute-start(bf16[208,384]{1,0:T(8,128)(2,1)S(1)} %get-tuple-element.92), channel_id=1, source_target_pairs={{5,0},{4,1},{7,2},{6,3},{1,4},{0,5},{3,6},{2,7},{13,8},{12,9},{15,... | collective-permute-start | bytes 479240 | tf_op jit(solution)/shard_map/cond/branch_1_fun/ppermute | solution.py:452
  44.2 9.3 %collective-permute-start.10 = (bf16[208,384]{1,0:T(8,128)(2,1)S(1)}, bf16[208,384]{1,0:T(8,128)(2,1)S(1)}, u32[]{:S(2)}, u32[]{:S(2)}) collective-permute-start(bf16[208,384]{1,0:T(8,128)(2,1)S(1)} %get-tuple-element.93), channel_id=1, source_target_pairs={{0,1},{1,0},{2,3},{3,2},{4,5},{5,4},{6,7},{7,6},{8,9},{9,8},{10,11... | collective-permute-start | bytes 479240 | tf_op jit(solution)/shard_map/cond/branch_1_fun/ppermute | solution.py:454
  45.7 8.9 %collective-permute-start.11 = (bf16[208,384]{1,0:T(8,128)(2,1)S(1)}, bf16[208,384]{1,0:T(8,128)(2,1)S(1)}, u32[]{:S(2)}, u32[]{:S(2)}) collective-permute-start(bf16[208,384]{1,0:T(8,128)(2,1)S(1)} %get-tuple-element.94), channel_id=1, source_target_pairs={{4,0},{6,2},{0,4},{2,6},{12,8},{14,10},{8,12},{10,14},{20,16},{22,... | collective-permute-start | bytes 479240 | tf_op jit(solution)/shard_map/cond/branch_1_fun/ppermute | solution.py:421
  55.7 0.7 %copy-start.2 = (bf16[192,768]{1,0:T(8,128)(2,1)}, bf16[192,768]{1,0:T(8,128)(2,1)S(1)}, u32[]{:S(2)}) copy-start(bf16[192,768]{1,0:T(8,128)(2,1)S(1)} %get-tuple-element.153) | copy-start | bytes 884740
where the time goes:
time: 56.2 us; the launch traced here: 56.4 us
  waiting for transfers between devices  26.7 us (48%)
  starting transfers between devices  14.2 us (25%)
  Pallas kernels  13.7 us (24%)
  between operations  0.76 us (1%)
  local copies, waits for them, and re-layouts  0.72 us (1%)
    ppermute x10, waiting for transfers between devices, moved(): return lax.ppermute(array, 'seq', pairs)  20.9 us
    ppermute x10, starting transfers between devices, moved(): return lax.ppermute(array, 'seq', pairs)  12.6 us
    pallas_call x6, Pallas kernels, attend(): pl.pallas_call(functools.partial(attend_kernel, which, places, arrays, no...  9.75 us
    ppermute x1, waiting for transfers between devices, merge(): over_both = lax.ppermute(over_both, ('seq', 'head'), pairs)  4.41 us
    ppermute x1, starting transfers between devices, merge(): over_x = lax.ppermute(over_x, 'head', [(0, 1), (1, 0)])  1.55 us
    ppermute x1, waiting for transfers between devices, merge(): over_x = lax.ppermute(over_x, 'head', [(0, 1), (1, 0)])  1.42 us
    pallas_call x1, Pallas kernels, pack(): pl.pallas_call(pack_kernel, out_shape=jax.ShapeDtypeStruct((2 * rows, col...  1.22 us
    pallas_call x1, Pallas kernels, meta(): pl.pallas_call(functools.partial(meta_kernel, halves), out_shape=[jax.Sha...  1.22 us
  transfers between devices with their start and end apart: 12, of which 7 were waited for; matrix products, arithmetic and copies ran while one was open for 0% of the time, Pallas kernels for 18%

commit v1 on v0

--- a/solution.py
+++ b/solution.py
@@ -150,7 +150,7 @@
     q_refs, refs = refs[:halves], refs[halves:]
     array_refs, refs = refs[: len(arrays)], refs[len(arrays) :]
     old_refs, refs = (None, refs) if fresh else (refs[:halves], refs[halves:])
-    new_refs, (held_q, held, state) = refs[:halves], refs[halves:]
+    new_refs, (held_q, held, state) = refs[:-3], refs[-3:]
     rows, columns = q_refs[0].shape
     tiles = rows // TILE
     count = held.shape[1] // 2 // TILE
@@ -243,11 +243,11 @@
 
     for half in range(halves):
         if brief:
-            new_refs[half][:columns] = state[half, :columns].astype(jnp.bfloat16)
-            statistics = state[half, columns:]
-            for n, part in enumerate(summands(statistics)):
-                at = columns + n * 2 * 8
-                new_refs[half][at : at + 2 * 8] = jnp.concatenate([part, part], axis=0)
+            at = half * new_refs[0].shape[0] // halves
+            new_refs[0][at : at + columns] = state[half, :columns].astype(jnp.bfloat16)
+            for n, part in enumerate(summands(state[half, columns:])):
+                row = at + columns + n * 2 * 8
+                new_refs[0][row : row + 2 * 8] = jnp.concatenate([part, part], axis=0)
         else:
             new_refs[half][...] = state[half]
 
@@ -262,12 +262,12 @@
     shape = jax.ShapeDtypeStruct((columns + -(-2 * heads // 8) * 8, rows), jnp.float32)
     arrays = list(enumerate(shifts or [None] * len(blocks)))
     pairs = halves * (rows // TILE) * heads * len(blocks) * (depth // 2 // TILE)
-    sent = jax.ShapeDtypeStruct((columns + 3 * 2 * 8, rows), jnp.bfloat16)
+    sent = jax.ShapeDtypeStruct((halves * (columns + 3 * 2 * 8), rows), jnp.bfloat16)
     return pl.pallas_call(
         functools.partial(attend_kernel, which, places, arrays, not states, unless_far, brief),
-        out_shape=[sent if brief else shape] * halves,
+        out_shape=[sent] if brief else [shape] * halves,
         in_specs=[VMEM] * (1 + halves + len(blocks) + len(states)),
-        out_specs=[VMEM] * halves,
+        out_specs=[VMEM] * (1 if brief else halves),
         scratch_shapes=[
             pltpu.VMEM((halves, rows, columns), queries[0].dtype),
             pltpu.VMEM((len(blocks), depth, columns), blocks[0].dtype),
@@ -313,48 +313,50 @@
 
 
 def message_kernel(*refs):
-    states, outs, held = refs[:4], refs[4:8], refs[8]
+    states, got_ref, outs, held = refs[:2], refs[2], refs[3:7], refs[7]
     rows = outs[0].shape[0] - 2 * 8
     columns = outs[0].shape[1]
     heads = columns // HEAD_DIM
     mine = lax.axis_index("head")
     for part in range(2):
-        pair, (keep_ref, send_ref) = states[2 * part : 2 * part + 2], outs[2 * part : 2 * part + 2]
+        ref, (keep_ref, send_ref) = states[part], outs[2 * part : 2 * part + 2]
+        at = part * got_ref.shape[0] // 2
         logs = []
-        rest = pair[1][columns:].astype(jnp.float32)
+        rest = got_ref[at + columns : at + got_ref.shape[0] // 2].astype(jnp.float32)
         statistics = functools.reduce(jnp.add, [rest[n * 2 * 8 : n * 2 * 8 + 8] for n in range(3)])
         for h in range(heads):
-            maxima = [pair[0][columns + h : columns + h + 1], statistics[h : h + 1]]
-            totals = [pair[0][columns + heads + h : columns + heads + h + 1], statistics[heads + h : heads + h + 1]]
+            maxima = [ref[columns + h : columns + h + 1], statistics[h : h + 1]]
+            totals = [ref[columns + heads + h : columns + heads + h + 1], statistics[heads + h : heads + h + 1]]
             largest = jnp.maximum(*maxima)
             factors = [jnp.exp2((m - largest) * SCALE2) for m in maxima]
             total = factors[0] * totals[0] + factors[1] * totals[1]
             some = jnp.where(total > 0, total, 1.0)
             scale = [f / some for f in factors]
             own = head_columns(h)
-            sums = pair[0][own] * scale[0] + pair[1][own].astype(jnp.float32) * scale[1]
+            got = got_ref[at + h * HEAD_DIM : at + (h + 1) * HEAD_DIM].astype(jnp.float32)
+            sums = ref[own] * scale[0] + got * scale[1]
             held[:, own] = sums.T.astype(held.dtype)
             log = jnp.where(total > 0, largest * SCALE2 + jnp.log2(some), LOWEST)
             logs += [part.astype(jnp.float32) for part in summands(log)]
         logs = jnp.concatenate(logs + [jnp.zeros((2 * 8 - len(logs), held.shape[0]), jnp.float32)], axis=0)
         later = pltpu.roll(logs, rows, 1)
-        for ref, which in ((send_ref, 1 - mine), (keep_ref, mine)):
-            ref[:rows] = held[pl.ds(pl.multiple_of(which * rows, 2 * 8), rows), :]
-            ref[rows:] = jnp.where(which == 0, logs, later).astype(ref.dtype)
-
-
-def messages(mine, peers):
-    rows, columns = mine[0].shape[1], mine[0].shape[0] // HEAD_DIM * HEAD_DIM
+        for out_ref, which in ((send_ref, 1 - mine), (keep_ref, mine)):
+            out_ref[:rows] = held[pl.ds(pl.multiple_of(which * rows, 2 * 8), rows), :]
+            out_ref[rows:] = jnp.where(which == 0, logs, later).astype(out_ref.dtype)
+
+
+def messages(mine, peer, got):
+    rows, columns = mine.shape[1], mine.shape[0] // HEAD_DIM * HEAD_DIM
     shape = jax.ShapeDtypeStruct((rows // 2 + 2 * 8, columns), jnp.bfloat16)
     return pl.pallas_call(
         message_kernel,
         out_shape=[shape] * 4,
-        in_specs=[VMEM] * 4,
+        in_specs=[VMEM] * 3,
         out_specs=[VMEM] * 4,
         scratch_shapes=[pltpu.VMEM((rows, columns), jnp.bfloat16)],
         compiler_params=params(),
         name="message",
-    )(*mine, *peers)
+    )(mine, peer, got)
 
 
 def settle_kernel(*refs):
@@ -444,10 +446,10 @@
     states = fold([b1], [B1], states, unless_far=True)
 
     def merge(blocks, places, states, shifts=None):
-        beside, diagonal = fold(blocks, places, states, which=[1, 3], shifts=shifts, brief=True)
-        beside, diagonal = moved(beside, sibling), moved(diagonal, sibling)
+        (others,) = fold(blocks, places, states, which=[1, 3], shifts=shifts, brief=True)
+        got = moved(others, sibling)
         mine, peer = fold(blocks, places, states, which=[0, 2], shifts=shifts)
-        keep, over_x, over_y, over_both = messages([mine, beside], [peer, diagonal])
+        keep, over_x, over_y, over_both = messages(mine, peer, got)
         pairs = [(2 * across(s) + 1 - x, 2 * s + x) for s in owners for x in range(2)]
         over_both = lax.ppermute(over_both, ("seq", "head"), pairs)
         over_y = moved(over_y, across)

time: 56.2 us -> 55.3 us (0.984); the launches traced: 56.4 us -> 54.7 us
  Pallas kernels: 13.7 us -> 11.1 us
  waiting for transfers between devices: 26.7 us -> 28.1 us
    pallas_call x6, Pallas kernels: 9.75 us -> 7.23 us  [attend(): pl.pallas_call(functools.partial(attend_kernel, which, places, arrays, no...]
    ppermute x10 -> x9, waiting for transfers between devices: 20.9 us -> 22.3 us  [moved(): return lax.ppermute(array, 'seq', pairs)]
    ppermute x1, starting transfers between devices: 0.07 us -> 0.66 us  [merge(): over_both = lax.ppermute(over_both, ('seq', 'head'), pairs)]
    ppermute x1, starting transfers between devices: 1.55 us -> 0.97 us  [merge(): over_x = lax.ppermute(over_x, 'head', [(0, 1), (1, 0)])]
    ppermute x10 -> x9, starting transfers between devices: 12.6 us -> 12.1 us  [moved(): return lax.ppermute(array, 'seq', pairs)]
  transfers between devices with their start and end apart: 12 -> 11, of which waited for: 7 -> 7; matrix products, arithmetic and copies ran while one was open for 0% -> 0% of each run, Pallas kernels for 18% -> 17%
where the time goes in v1:
time: 55.3 us; the launch traced here: 54.7 us
  waiting for transfers between devices  28.1 us (51%)
  starting transfers between devices  13.7 us (25%)
  Pallas kernels  11.1 us (20%)
  between operations  0.76 us (1%)
  local copies, waits for them, and re-layouts  0.72 us (1%)
    ppermute x9, waiting for transfers between devices, moved(): return lax.ppermute(array, 'seq', pairs)  22.3 us
    ppermute x9, starting transfers between devices, moved(): return lax.ppermute(array, 'seq', pairs)  12.1 us
    pallas_call x6, Pallas kernels, attend(): pl.pallas_call(functools.partial(attend_kernel, which, places, arrays, no...  7.23 us
    ppermute x1, waiting for transfers between devices, merge(): over_both = lax.ppermute(over_both, ('seq', 'head'), pairs)  4.41 us
    ppermute x1, waiting for transfers between devices, merge(): over_x = lax.ppermute(over_x, 'head', [(0, 1), (1, 0)])  1.42 us
    pallas_call x1, Pallas kernels, pack(): pl.pallas_call(pack_kernel, out_shape=jax.ShapeDtypeStruct((2 * rows, col...  1.22 us
    pallas_call x1, Pallas kernels, meta(): pl.pallas_call(functools.partial(meta_kernel, halves), out_shape=[jax.Sha...  1.22 us
  transfers between devices with their start and end apart: 11, of which 7 were waited for; matrix products, arithmetic and copies ran while one was open for 0% of the time, Pallas kernels for 17%

profile of v1, /device:TPU:0, one launch (start us, length us, event | category | flops | bytes accessed | tf_op | source)
XLA Modules:
  0.0 54.7 jit_solution(13922665161018676229)
XLA Ops:
  0.0 0.0 copy-start.1
  0.0 0.0 copy-start
  0.0 3.0 %collective-permute-start.10 = (bf16[384,384]{1,0:T(8,128)(2,1)}, bf16[384,384]{1,0:T(8,128)(2,1)S(1)}, u32[]{:S(2)}, u32[]{:S(2)}) collective-permute-start(bf16[384,384]{1,0:T(8,128)(2,1)} %refs_0_.3), channel_id=1, source_target_pairs={{4,0},{6,2},{0,4},{2,6},{12,8},{14,10},{8,12},{10,14},{20,16},{22,... | collective-permute-start | bytes 884744 | tf_op jit(solution)/shard_map/ppermute | solution.py:423
  3.0 1.2 %pack.1.refs_2_ = bf16[768,384]{1,0:T(8,128)(2,1)S(1)} custom-call(bf16[384,384]{1,0:T(8,128)(2,1)} %k_ref.1, bf16[384,384]{1,0:T(8,128)(2,1)} %v_ref.1), custom_call_target="tpu_custom_call" | custom-call | tf_op jit(solution)/shard_map/pack/pallas_call | solution.py:100
  4.2 3.5 %collective-permute-start.14 = (bf16[768,384]{1,0:T(8,128)(2,1)S(1)}, bf16[768,384]{1,0:T(8,128)(2,1)S(1)}, u32[]{:S(2)}, u32[]{:S(2)}) collective-permute-start(bf16[768,384]{1,0:T(8,128)(2,1)S(1)} %pack.1.refs_2_), channel_id=1, source_target_pairs={{10,2},{12,4},{0,8},{18,10},{20,12},{6,14},{8,16},{26,18},{28,20},... | collective-permute-start | bytes 1769480 | tf_op jit(solution)/shard_map/ppermute | solution.py:423
  7.7 1.3 %collective-permute-start.11 = (bf16[768,384]{1,0:T(8,128)(2,1)S(1)}, bf16[768,384]{1,0:T(8,128)(2,1)S(1)}, u32[]{:S(2)}, u32[]{:S(2)}) collective-permute-start(bf16[768,384]{1,0:T(8,128)(2,1)S(1)} %pack.1.refs_2_), channel_id=1, source_target_pairs={{8,0},{14,6},{16,8},{2,10},{4,12},{22,14},{24,16},{10,18},{12,20},... | collective-permute-start | bytes 1769480 | tf_op jit(solution)/shard_map/ppermute | solution.py:423
  9.0 0.0 copy-done.1
  9.0 0.1 collective-permute-start.12
  9.2 1.1 %collective-permute-done.10.refs_0_.refs_2_ = bf16[384,384]{1,0:T(8,128)(2,1)S(1)} collective-permute-done((bf16[384,384]{1,0:T(8,128)(2,1)}, bf16[384,384]{1,0:T(8,128)(2,1)S(1)}, u32[]{:S(2)}, u32[]{:S(2)}) %collective-permute-start.10) | collective-permute-done | bytes 294944 | tf_op jit(solution)/shard_map/ppermute | solution.py:423
  10.3 0.0 collective-permute-start.13
  10.3 0.0 copy-done
  10.3 1.2 %meta.1 = (s32[16,384]{1,0:T(8,128)S(1)}, s32[1]{0:T(128)}) custom-call(s32[5]{0:T(128)S(1)} %copy-done), custom_call_target="tpu_custom_call" | custom-call | flops 268435456 | tf_op jit(solution)/shard_map/meta/pallas_call | solution.py:69
  12.1 0.0 collective-permute-done.12.refs_1_
  12.1 2.0 %attend.13 = (f32[392,384]{1,0:T(8,128)S(1)}, f32[392,384]{1,0:T(8,128)S(1)}) custom-call(s32[16,384]{1,0:T(8,128)S(1)} %get-tuple-element.103.bounds_ref, bf16[384,384]{1,0:T(8,128)(2,1)S(1)} %copy-done.1, bf16[384,384]{1,0:T(8,128)(2,1)S(1)} %collective-permute-done.12.refs_1_, bf16[768,384]{1,0:T(8,128)(2,1)S(1)} %pack.1.refs_2_), custom_call_target="tpu_custom_call" | custom-call | flops 452984832 | bytes 1769472 | tf_op jit(solution)/shard_map/attend/pallas_call | solution.py:266
  14.2 0.0 collective-permute-done.13.refs_1_.refs_3_
  14.2 1.2 %attend.14 = (f32[392,384]{1,0:T(8,128)S(1)}, f32[392,384]{1,0:T(8,128)S(1)}) custom-call(s32[16,384]{1,0:T(8,128)S(1)} %get-tuple-element.103.bounds_ref, bf16[384,384]{1,0:T(8,128)(2,1)S(1)} %collective-permute-done.10.refs_0_.refs_2_, bf16[384,384]{1,0:T(8,128)(2,1)S(1)} %collective-permute-done.13.refs_1_.refs_3_, bf16[768,384]{1,0:T(8,128)(2,1)S(1)} %pack.1.refs_2_), custom_call_target="tpu_custom_call" | custom-call | flops 452984832 | bytes 1769472 | tf_op jit(solution)/shard_map/attend/pallas_call | solution.py:266
  15.3 5.4 %collective-permute-done.14.refs_4_ = bf16[768,384]{1,0:T(8,128)(2,1)S(1)} collective-permute-done((bf16[768,384]{1,0:T(8,128)(2,1)S(1)}, bf16[768,384]{1,0:T(8,128)(2,1)S(1)}, u32[]{:S(2)}, u32[]{:S(2)}) %collective-permute-start.14) | collective-permute-done | bytes 589856 | tf_op jit(solution)/shard_map/ppermute | solution.py:423
  20.8 0.6 %attend.15 = (f32[392,384]{1,0:T(8,128)S(1)}, f32[392,384]{1,0:T(8,128)S(1)}, f32[392,384]{1,0:T(8,128)S(1)}, f32[392,384]{1,0:T(8,128)S(1)}) custom-call(s32[16,384]{1,0:T(8,128)S(1)} %get-tuple-element.103.bounds_ref, bf16[384,384]{1,0:T(8,128)(2,1)S(1)} %copy-done.1, bf16[384,384]{1,0:T(8,128)(2,1)S(1)} %collective-permute-done.12.refs_1_, ...), custom_call_target="tpu_custom_call" | custom-call | flops 905969664 | bytes 2949120 | tf_op jit(solution)/shard_map/attend/pallas_call | solution.py:266
  21.4 0.0 collective-permute-done.11
  21.4 32.6 %conditional.1 = (bf16[192,768]{1,0:T(8,128)(2,1)S(1)}) conditional(s32[]{:T(128)} %bitcast, (s32[16,384]{1,0:T(8,128)S(1)}, bf16[384,384]{1,0:T(8,128)(2,1)S(1)}, bf16[384,384]{1,0:T(8,128)(2,1)S(1)}, bf16[768,384]{1,0:T(8,128)(2,1)S(1)}, f32[392,384]{1,0:T(8,128)S(1)}, /*index=5*/f32[392,384]{1,0:T(8,128)S(1)}, bf16[384,384]{1,0:T(8,128)(2,1)S(1)}, ...), branch_computations={%region_0.0_spmd, %region_1.0_spmd} | conditional | flops 3623878656 | bytes 16761080 | solution.py:468
  21.4 0.1 onward.1
  21.5 1.3 %collective-permute-start.4 = (bf16[768,384]{1,0:T(8,128)(2,1)S(1)}, bf16[768,384]{1,0:T(8,128)(2,1)S(1)}, u32[]{:S(2)}, u32[]{:S(2)}) collective-permute-start(bf16[768,384]{1,0:T(8,128)(2,1)S(1)} %get-tuple-element.74), channel_id=1, source_target_pairs={{8,0},{10,2},{16,8},{18,10},{4,12},{6,14},{24,16},{26,18},{12,20},... | collective-permute-start | bytes 1769480 | tf_op jit(solution)/shard_map/cond/branch_1_fun/ppermute | solution.py:423
  22.8 0.9 %collective-permute-start.5 = (bf16[512,384]{1,0:T(8,128)(2,1)S(1)}, bf16[512,384]{1,0:T(8,128)(2,1)S(1)}, u32[]{:S(2)}, u32[]{:S(2)}) collective-permute-start(bf16[512,384]{1,0:T(8,128)(2,1)S(1)} %get-tuple-element.75), channel_id=1, source_target_pairs={{12,4},{2,10},{20,12},{10,18},{28,20},{18,26},{13,5},{3,11},{21,13... | collective-permute-start | bytes 1179656 | tf_op jit(solution)/shard_map/cond/branch_1_fun/ppermute | solution.py:423
  23.7 2.5 %attend.10 = (f32[392,384]{1,0:T(8,128)S(1)}, f32[392,384]{1,0:T(8,128)S(1)}, f32[392,384]{1,0:T(8,128)S(1)}, f32[392,384]{1,0:T(8,128)S(1)}) custom-call(s32[16,384]{1,0:T(8,128)S(1)} %get-tuple-element.68.bounds_ref, bf16[384,384]{1,0:T(8,128)(2,1)S(1)} %get-tuple-element.69.refs_0_, bf16[384,384]{1,0:T(8,128)(2,1)S(1)} %get-tuple-element.76.refs_1_.refs_0_, ...), custom_call_target="tpu_custom_call" | custom-call | flops 1811939328 | bytes 3538944 | tf_op jit(solution)/shard_map/cond/branch_1_fun/attend/pallas_call | solution.py:266
  26.2 0.0 collective-permute-done.5.refs_3_
  26.2 13.0 %collective-permute-done.4.refs_2_ = bf16[768,384]{1,0:T(8,128)(2,1)S(1)} collective-permute-done((bf16[768,384]{1,0:T(8,128)(2,1)S(1)}, bf16[768,384]{1,0:T(8,128)(2,1)S(1)}, u32[]{:S(2)}, u32[]{:S(2)}) %collective-permute-start.4) | collective-permute-done | bytes 589856 | tf_op jit(solution)/shard_map/cond/branch_1_fun/ppermute | solution.py:423
  39.2 0.5 attend.12
  39.7 0.1 collective-permute-start.6
  39.7 0.5 attend.11
  40.2 1.6 %collective-permute-done.6.refs_2_ = bf16[864,384]{1,0:T(8,128)(2,1)S(1)} collective-permute-done((bf16[864,384]{1,0:T(8,128)(2,1)S(1)}, bf16[864,384]{1,0:T(8,128)(2,1)S(1)}, u32[]{:S(2)}, u32[]{:S(2)}) %collective-permute-start.6) | collective-permute-done | bytes 663584 | tf_op jit(solution)/shard_map/cond/branch_1_fun/ppermute | solution.py:423
  41.8 0.6 %message.3 = (bf16[208,384]{1,0:T(8,128)(2,1)S(1)}, bf16[208,384]{1,0:T(8,128)(2,1)S(1)}, bf16[208,384]{1,0:T(8,128)(2,1)S(1)}, bf16[208,384]{1,0:T(8,128)(2,1)S(1)}) custom-call(f32[392,384]{1,0:T(8,128)S(1)} %get-tuple-element.84.refs_0_, f32[392,384]{1,0:T(8,128)S(1)} %get-tuple-element.85.refs_1_, bf16[864,384]{1,0:T(8,128)(2,1)S(1)} %collective-permute-done.6.refs_2_), custom_call_target="tpu_custom_call" | custom-call | tf_op jit(solution)/shard_map/cond/branch_1_fun/message/pallas_call | solution.py:351
  42.4 0.7 %collective-permute-start.7 = (bf16[208,384]{1,0:T(8,128)(2,1)S(1)}, bf16[208,384]{1,0:T(8,128)(2,1)S(1)}, u32[]{:S(2)}, u32[]{:S(2)}) collective-permute-start(bf16[208,384]{1,0:T(8,128)(2,1)S(1)} %get-tuple-element.88), channel_id=1, source_target_pairs={{5,0},{4,1},{7,2},{6,3},{1,4},{0,5},{3,6},{2,7},{13,8},{12,9},{15,... | collective-permute-start | bytes 479240 | tf_op jit(solution)/shard_map/cond/branch_1_fun/ppermute | solution.py:454
  43.1 1.0 %collective-permute-start.8 = (bf16[208,384]{1,0:T(8,128)(2,1)S(1)}, bf16[208,384]{1,0:T(8,128)(2,1)S(1)}, u32[]{:S(2)}, u32[]{:S(2)}) collective-permute-start(bf16[208,384]{1,0:T(8,128)(2,1)S(1)} %get-tuple-element.89), channel_id=1, source_target_pairs={{0,1},{1,0},{2,3},{3,2},{4,5},{5,4},{6,7},{7,6},{8,9},{9,8},{10,11... | collective-permute-start | bytes 479240 | tf_op jit(solution)/shard_map/cond/branch_1_fun/ppermute | solution.py:456
  44.0 1.9 %collective-permute-start.9 = (bf16[208,384]{1,0:T(8,128)(2,1)S(1)}, bf16[208,384]{1,0:T(8,128)(2,1)S(1)}, u32[]{:S(2)}, u32[]{:S(2)}) collective-permute-start(bf16[208,384]{1,0:T(8,128)(2,1)S(1)} %get-tuple-element.90), channel_id=1, source_target_pairs={{4,0},{6,2},{0,4},{2,6},{12,8},{14,10},{8,12},{10,14},{20,16},{22,... | collective-permute-start | bytes 479240 | tf_op jit(solution)/shard_map/cond/branch_1_fun/ppermute | solution.py:423
  46.0 4.4 %collective-permute-done.7.refs_0_ = bf16[208,384]{1,0:T(8,128)(2,1)S(1)} collective-permute-done((bf16[208,384]{1,0:T(8,128)(2,1)S(1)}, bf16[208,384]{1,0:T(8,128)(2,1)S(1)}, u32[]{:S(2)}, u32[]{:S(2)}) %collective-permute-start.7) | collective-permute-done | bytes 159776 | tf_op jit(solution)/shard_map/cond/branch_1_fun/ppermute | solution.py:454
  50.4 1.4 %collective-permute-done.8.refs_1_ = bf16[208,384]{1,0:T(8,128)(2,1)S(1)} collective-permute-done((bf16[208,384]{1,0:T(8,128)(2,1)S(1)}, bf16[208,384]{1,0:T(8,128)(2,1)S(1)}, u32[]{:S(2)}, u32[]{:S(2)}) %collective-permute-start.8) | collective-permute-done | bytes 159776 | tf_op jit(solution)/shard_map/cond/branch_1_fun/ppermute | solution.py:456
  51.8 1.2 %collective-permute-done.9.refs_2_ = bf16[208,384]{1,0:T(8,128)(2,1)S(1)} collective-permute-done((bf16[208,384]{1,0:T(8,128)(2,1)S(1)}, bf16[208,384]{1,0:T(8,128)(2,1)S(1)}, u32[]{:S(2)}, u32[]{:S(2)}) %collective-permute-start.9) | collective-permute-done | bytes 159776 | tf_op jit(solution)/shard_map/cond/branch_1_fun/ppermute | solution.py:423
  52.9 0.8 %settle.3 = bf16[192,768]{1,0:T(8,128)(2,1)S(1)} custom-call(bf16[208,384]{1,0:T(8,128)(2,1)S(1)} %collective-permute-done.7.refs_0_, bf16[208,384]{1,0:T(8,128)(2,1)S(1)} %collective-permute-done.8.refs_1_, bf16[208,384]{1,0:T(8,128)(2,1)S(1)} %collective-permute-done.9.refs_2_, bf16[208,384]{1,0:T(8,128)(2,1)S(1)} %get-tuple-element.91.refs_3_), custom_call_target="tpu_custom_call" | custom-call | tf_op jit(solution)/shard_map/cond/branch_1_fun/settle/pallas_call | solution.py:388
  54.0 0.0 copy-start.2
  54.0 0.7 %copy-done.2 = bf16[192,768]{1,0:T(8,128)(2,1)} copy-done((bf16[192,768]{1,0:T(8,128)(2,1)}, bf16[192,768]{1,0:T(8,128)(2,1)S(1)}, u32[]{:S(2)}) %copy-start.2) | copy-done | bytes 294936
Async XLA Ops:
  0.0 9.0 %copy-start.1 = (bf16[384,384]{1,0:T(8,128)(2,1)S(1)}, bf16[384,384]{1,0:T(8,128)(2,1)}, u32[]{:S(2)}) copy-start(bf16[384,384]{1,0:T(8,128)(2,1)} %refs_0_.3) | copy-start | bytes 884740
  0.0 10.3 %copy-start = (s32[5]{0:T(128)S(1)}, s32[5]{0:T(128)}, u32[]{:S(2)}) copy-start(s32[5]{0:T(128)} %tiles_ref.1) | copy-start | bytes 64
  0.0 10.3 %collective-permute-start.10 = (bf16[384,384]{1,0:T(8,128)(2,1)}, bf16[384,384]{1,0:T(8,128)(2,1)S(1)}, u32[]{:S(2)}, u32[]{:S(2)}) collective-permute-start(bf16[384,384]{1,0:T(8,128)(2,1)} %refs_0_.3), channel_id=1, source_target_pairs={{4,0},{6,2},{0,4},{2,6},{12,8},{14,10},{8,12},{10,14},{20,16},{22,... | collective-permute-start | bytes 884744 | tf_op jit(solution)/shard_map/ppermute | solution.py:423
  4.2 16.6 %collective-permute-start.14 = (bf16[768,384]{1,0:T(8,128)(2,1)S(1)}, bf16[768,384]{1,0:T(8,128)(2,1)S(1)}, u32[]{:S(2)}, u32[]{:S(2)}) collective-permute-start(bf16[768,384]{1,0:T(8,128)(2,1)S(1)} %pack.1.refs_2_), channel_id=1, source_target_pairs={{10,2},{12,4},{0,8},{18,10},{20,12},{6,14},{8,16},{26,18},{28,20},... | collective-permute-start | bytes 1769480 | tf_op jit(solution)/shard_map/ppermute | solution.py:423
  7.7 13.7 %collective-permute-start.11 = (bf16[768,384]{1,0:T(8,128)(2,1)S(1)}, bf16[768,384]{1,0:T(8,128)(2,1)S(1)}, u32[]{:S(2)}, u32[]{:S(2)}) collective-permute-start(bf16[768,384]{1,0:T(8,128)(2,1)S(1)} %pack.1.refs_2_), channel_id=1, source_target_pairs={{8,0},{14,6},{16,8},{2,10},{4,12},{22,14},{24,16},{10,18},{12,20},... | collective-permute-start | bytes 1769480 | tf_op jit(solution)/shard_map/ppermute | solution.py:423
  9.0 3.1 %collective-permute-start.12 = (bf16[384,384]{1,0:T(8,128)(2,1)S(1)}, bf16[384,384]{1,0:T(8,128)(2,1)S(1)}, u32[]{:S(2)}, u32[]{:S(2)}) collective-permute-start(bf16[384,384]{1,0:T(8,128)(2,1)S(1)} %copy-done.1), channel_id=1, source_target_pairs={{2,0},{0,2},{6,4},{4,6},{10,8},{8,10},{14,12},{12,14},{18,16},{16,... | collective-permute-start | bytes 884744 | tf_op jit(solution)/shard_map/ppermute | solution.py:423
  10.3 3.9 %collective-permute-start.13 = (bf16[384,384]{1,0:T(8,128)(2,1)S(1)}, bf16[384,384]{1,0:T(8,128)(2,1)S(1)}, u32[]{:S(2)}, u32[]{:S(2)}) collective-permute-start(bf16[384,384]{1,0:T(8,128)(2,1)S(1)} %collective-permute-done.10.refs_0_.refs_2_), channel_id=1, source_target_pairs={{2,0},{0,2},{6,4},{4,6},{10,8},{8,10},{14,12},{12,14},{18,16},{16,... | collective-permute-start | bytes 884744 | tf_op jit(solution)/shard_map/ppermute | solution.py:423
  21.5 17.6 %collective-permute-start.4 = (bf16[768,384]{1,0:T(8,128)(2,1)S(1)}, bf16[768,384]{1,0:T(8,128)(2,1)S(1)}, u32[]{:S(2)}, u32[]{:S(2)}) collective-permute-start(bf16[768,384]{1,0:T(8,128)(2,1)S(1)} %get-tuple-element.74), channel_id=1, source_target_pairs={{8,0},{10,2},{16,8},{18,10},{4,12},{6,14},{24,16},{26,18},{12,20},... | collective-permute-start | bytes 1769480 | tf_op jit(solution)/shard_map/cond/branch_1_fun/ppermute | solution.py:423
  22.8 3.4 %collective-permute-start.5 = (bf16[512,384]{1,0:T(8,128)(2,1)S(1)}, bf16[512,384]{1,0:T(8,128)(2,1)S(1)}, u32[]{:S(2)}, u32[]{:S(2)}) collective-permute-start(bf16[512,384]{1,0:T(8,128)(2,1)S(1)} %get-tuple-element.75), channel_id=1, source_target_pairs={{12,4},{2,10},{20,12},{10,18},{28,20},{18,26},{13,5},{3,11},{21,13... | collective-permute-start | bytes 1179656 | tf_op jit(solution)/shard_map/cond/branch_1_fun/ppermute | solution.py:423
  39.7 2.2 %collective-permute-start.6 = (bf16[864,384]{1,0:T(8,128)(2,1)S(1)}, bf16[864,384]{1,0:T(8,128)(2,1)S(1)}, u32[]{:S(2)}, u32[]{:S(2)}) collective-permute-start(bf16[864,384]{1,0:T(8,128)(2,1)S(1)} %attend.12), channel_id=1, source_target_pairs={{2,0},{0,2},{6,4},{4,6},{10,8},{8,10},{14,12},{12,14},{18,16},{16,... | collective-permute-start | bytes 1990664 | tf_op jit(solution)/shard_map/cond/branch_1_fun/ppermute | solution.py:423
  42.4 8.0 %collective-permute-start.7 = (bf16[208,384]{1,0:T(8,128)(2,1)S(1)}, bf16[208,384]{1,0:T(8,128)(2,1)S(1)}, u32[]{:S(2)}, u32[]{:S(2)}) collective-permute-start(bf16[208,384]{1,0:T(8,128)(2,1)S(1)} %get-tuple-element.88), channel_id=1, source_target_pairs={{5,0},{4,1},{7,2},{6,3},{1,4},{0,5},{3,6},{2,7},{13,8},{12,9},{15,... | collective-permute-start | bytes 479240 | tf_op jit(solution)/shard_map/cond/branch_1_fun/ppermute | solution.py:454
  43.1 8.7 %collective-permute-start.8 = (bf16[208,384]{1,0:T(8,128)(2,1)S(1)}, bf16[208,384]{1,0:T(8,128)(2,1)S(1)}, u32[]{:S(2)}, u32[]{:S(2)}) collective-permute-start(bf16[208,384]{1,0:T(8,128)(2,1)S(1)} %get-tuple-element.89), channel_id=1, source_target_pairs={{0,1},{1,0},{2,3},{3,2},{4,5},{5,4},{6,7},{7,6},{8,9},{9,8},{10,11... | collective-permute-start | bytes 479240 | tf_op jit(solution)/shard_map/cond/branch_1_fun/ppermute | solution.py:456
  44.0 8.9 %collective-permute-start.9 = (bf16[208,384]{1,0:T(8,128)(2,1)S(1)}, bf16[208,384]{1,0:T(8,128)(2,1)S(1)}, u32[]{:S(2)}, u32[]{:S(2)}) collective-permute-start(bf16[208,384]{1,0:T(8,128)(2,1)S(1)} %get-tuple-element.90), channel_id=1, source_target_pairs={{4,0},{6,2},{0,4},{2,6},{12,8},{14,10},{8,12},{10,14},{20,16},{22,... | collective-permute-start | bytes 479240 | tf_op jit(solution)/shard_map/cond/branch_1_fun/ppermute | solution.py:423
  54.0 0.7 %copy-start.2 = (bf16[192,768]{1,0:T(8,128)(2,1)}, bf16[192,768]{1,0:T(8,128)(2,1)S(1)}, u32[]{:S(2)}) copy-start(bf16[192,768]{1,0:T(8,128)(2,1)S(1)} %get-tuple-element.145) | copy-start | bytes 884740

commit v2 on v1

--- a/solution.py
+++ b/solution.py
@@ -14,7 +14,7 @@
 
 LOWEST = -1e30
 SCALE2 = math.log2(math.e) / math.sqrt(HEAD_DIM)
-COST = 1
+COST = 2
 
 VMEM = pl.BlockSpec(memory_space=pltpu.VMEM)
 SMEM = pl.BlockSpec(memory_space=pltpu.SMEM)

time: 55.3 us -> 38.9 us (0.70)
  waiting for transfers between devices: 28.1 us -> 11.5 us
  Pallas kernels: 11.1 us -> 12.5 us
    ppermute x9 -> x7, waiting for transfers between devices: 22.3 us -> 4.6 us  [moved(): return lax.ppermute(array, 'seq', pairs)]
    ppermute x1, starting transfers between devices: 0.66 us -> 3.29 us  [merge(): over_both = lax.ppermute(over_both, ('seq', 'head'), pairs)]
    ppermute x9 -> x7, starting transfers between devices: 12.1 us -> 9.89 us  [moved(): return lax.ppermute(array, 'seq', pairs)]
    pallas_call x6 -> x5, Pallas kernels: 7.23 us -> 8.65 us  [attend(): pl.pallas_call(functools.partial(attend_kernel, which, places, arrays, no...]
    ppermute x1, waiting for transfers between devices: 1.42 us -> 2.52 us  [merge(): over_x = lax.ppermute(over_x, 'head', [(0, 1), (1, 0)])]
    ppermute x1, starting transfers between devices: 0.97 us -> 0.01 us  [merge(): over_x = lax.ppermute(over_x, 'head', [(0, 1), (1, 0)])]
  transfers between devices with their start and end apart: 11 -> 9, of which waited for: 7 -> 7; matrix products, arithmetic and copies ran while one was open for 0% -> 0% of each run, Pallas kernels for 17% -> 23%
where the time goes in v2:
time: 38.9 us; the launch traced here: 38.8 us
  starting transfers between devices  13.2 us (34%)
  Pallas kernels  12.5 us (32%)
  waiting for transfers between devices  11.5 us (30%)
  between operations  0.76 us (2%)
  local copies, waits for them, and re-layouts  0.72 us (2%)
    ppermute x7, starting transfers between devices, moved(): return lax.ppermute(array, 'seq', pairs)  9.89 us
    pallas_call x5, Pallas kernels, attend(): pl.pallas_call(functools.partial(attend_kernel, which, places, arrays, no...  8.65 us
    ppermute x7, waiting for transfers between devices, moved(): return lax.ppermute(array, 'seq', pairs)  4.6 us
    ppermute x1, waiting for transfers between devices, merge(): over_both = lax.ppermute(over_both, ('seq', 'head'), pairs)  4.35 us
    ppermute x1, starting transfers between devices, merge(): over_both = lax.ppermute(over_both, ('seq', 'head'), pairs)  3.29 us
    ppermute x1, waiting for transfers between devices, merge(): over_x = lax.ppermute(over_x, 'head', [(0, 1), (1, 0)])  2.52 us
    pallas_call x1, Pallas kernels, pack(): pl.pallas_call(pack_kernel, out_shape=jax.ShapeDtypeStruct((2 * rows, col...  1.22 us
    pallas_call x1, Pallas kernels, meta(): pl.pallas_call(functools.partial(meta_kernel, halves), out_shape=[jax.Sha...  1.22 us
  transfers between devices with their start and end apart: 9, of which 7 were waited for; matrix products, arithmetic and copies ran while one was open for 0% of the time, Pallas kernels for 23%

profile of v2, /device:TPU:0, one launch (start us, length us, event | category | flops | bytes accessed | tf_op | source)
XLA Modules:
  0.0 38.8 jit_solution(13299711940624049539)
XLA Ops:
  0.0 0.0 copy-start.2
  0.0 0.0 copy-start
  0.0 3.0 %collective-permute-start.10 = (bf16[384,384]{1,0:T(8,128)(2,1)}, bf16[384,384]{1,0:T(8,128)(2,1)S(1)}, u32[]{:S(2)}, u32[]{:S(2)}) collective-permute-start(bf16[384,384]{1,0:T(8,128)(2,1)} %refs_0_.3), channel_id=1, source_target_pairs={{4,0},{6,2},{0,4},{2,6},{12,8},{14,10},{8,12},{10,14},{20,16},{22,... | collective-permute-start | bytes 884744 | tf_op jit(solution)/shard_map/ppermute | solution.py:423
  3.0 1.2 %pack.1.refs_2_ = bf16[768,384]{1,0:T(8,128)(2,1)S(1)} custom-call(bf16[384,384]{1,0:T(8,128)(2,1)} %k_ref.1, bf16[384,384]{1,0:T(8,128)(2,1)} %v_ref.1), custom_call_target="tpu_custom_call" | custom-call | tf_op jit(solution)/shard_map/pack/pallas_call | solution.py:100
  4.2 3.5 %collective-permute-start.14 = (bf16[768,384]{1,0:T(8,128)(2,1)S(1)}, bf16[768,384]{1,0:T(8,128)(2,1)S(1)}, u32[]{:S(2)}, u32[]{:S(2)}) collective-permute-start(bf16[768,384]{1,0:T(8,128)(2,1)S(1)} %pack.1.refs_2_), channel_id=1, source_target_pairs={{10,2},{12,4},{0,8},{18,10},{20,12},{6,14},{8,16},{26,18},{28,20},... | collective-permute-start | bytes 1769480 | tf_op jit(solution)/shard_map/ppermute | solution.py:423
  7.7 0.0 copy-done.2
  7.7 0.1 collective-permute-start.12
  7.8 1.3 %collective-permute-start.11 = (bf16[768,384]{1,0:T(8,128)(2,1)S(1)}, bf16[768,384]{1,0:T(8,128)(2,1)S(1)}, u32[]{:S(2)}, u32[]{:S(2)}) collective-permute-start(bf16[768,384]{1,0:T(8,128)(2,1)S(1)} %pack.1.refs_2_), channel_id=1, source_target_pairs={{8,0},{14,6},{16,8},{2,10},{4,12},{22,14},{24,16},{10,18},{12,20},... | collective-permute-start | bytes 1769480 | tf_op jit(solution)/shard_map/ppermute | solution.py:423
  9.1 1.1 %collective-permute-done.10.refs_0_.refs_2_ = bf16[384,384]{1,0:T(8,128)(2,1)S(1)} collective-permute-done((bf16[384,384]{1,0:T(8,128)(2,1)}, bf16[384,384]{1,0:T(8,128)(2,1)S(1)}, u32[]{:S(2)}, u32[]{:S(2)}) %collective-permute-start.10) | collective-permute-done | bytes 294944 | tf_op jit(solution)/shard_map/ppermute | solution.py:423
  10.3 1.3 %collective-permute-start.13 = (bf16[384,384]{1,0:T(8,128)(2,1)S(1)}, bf16[384,384]{1,0:T(8,128)(2,1)S(1)}, u32[]{:S(2)}, u32[]{:S(2)}) collective-permute-start(bf16[384,384]{1,0:T(8,128)(2,1)S(1)} %collective-permute-done.10.refs_0_.refs_2_), channel_id=1, source_target_pairs={{2,0},{0,2},{6,4},{4,6},{10,8},{8,10},{14,12},{12,14},{18,16},{16,... | collective-permute-start | bytes 884744 | tf_op jit(solution)/shard_map/ppermute | solution.py:423
  11.6 0.0 copy-done
  11.6 1.2 %meta.1 = (s32[16,384]{1,0:T(8,128)S(1)}, s32[1]{0:T(128)}) custom-call(s32[5]{0:T(128)S(1)} %copy-done), custom_call_target="tpu_custom_call" | custom-call | flops 536870912 | tf_op jit(solution)/shard_map/meta/pallas_call | solution.py:69
  13.5 0.0 collective-permute-done.12.refs_1_
  13.5 2.0 %attend.13 = (f32[392,384]{1,0:T(8,128)S(1)}, f32[392,384]{1,0:T(8,128)S(1)}) custom-call(s32[16,384]{1,0:T(8,128)S(1)} %get-tuple-element.103.bounds_ref, bf16[384,384]{1,0:T(8,128)(2,1)S(1)} %copy-done.2, bf16[384,384]{1,0:T(8,128)(2,1)S(1)} %collective-permute-done.12.refs_1_, bf16[768,384]{1,0:T(8,128)(2,1)S(1)} %pack.1.refs_2_), custom_call_target="tpu_custom_call" | custom-call | flops 905969664 | bytes 1769472 | tf_op jit(solution)/shard_map/attend/pallas_call | solution.py:266
  15.5 0.0 collective-permute-done.13.refs_1_.refs_3_
  15.5 2.0 %attend.14 = (f32[392,384]{1,0:T(8,128)S(1)}, f32[392,384]{1,0:T(8,128)S(1)}) custom-call(s32[16,384]{1,0:T(8,128)S(1)} %get-tuple-element.103.bounds_ref, bf16[384,384]{1,0:T(8,128)(2,1)S(1)} %collective-permute-done.10.refs_0_.refs_2_, bf16[384,384]{1,0:T(8,128)(2,1)S(1)} %collective-permute-done.13.refs_1_.refs_3_, bf16[768,384]{1,0:T(8,128)(2,1)S(1)} %pack.1.refs_2_), custom_call_target="tpu_custom_call" | custom-call | flops 905969664 | bytes 1769472 | tf_op jit(solution)/shard_map/attend/pallas_call | solution.py:266
  17.5 0.7 %collective-permute-done.14.refs_4_ = bf16[768,384]{1,0:T(8,128)(2,1)S(1)} collective-permute-done((bf16[768,384]{1,0:T(8,128)(2,1)S(1)}, bf16[768,384]{1,0:T(8,128)(2,1)S(1)}, u32[]{:S(2)}, u32[]{:S(2)}) %collective-permute-start.14) | collective-permute-done | bytes 589856 | tf_op jit(solution)/shard_map/ppermute | solution.py:423
  18.2 0.6 %attend.15 = (f32[392,384]{1,0:T(8,128)S(1)}, f32[392,384]{1,0:T(8,128)S(1)}, f32[392,384]{1,0:T(8,128)S(1)}, f32[392,384]{1,0:T(8,128)S(1)}) custom-call(s32[16,384]{1,0:T(8,128)S(1)} %get-tuple-element.103.bounds_ref, bf16[384,384]{1,0:T(8,128)(2,1)S(1)} %copy-done.2, bf16[384,384]{1,0:T(8,128)(2,1)S(1)} %collective-permute-done.12.refs_1_, ...), custom_call_target="tpu_custom_call" | custom-call | flops 1811939328 | bytes 2949120 | tf_op jit(solution)/shard_map/attend/pallas_call | solution.py:266
  18.9 2.0 %collective-permute-done.11 = bf16[768,384]{1,0:T(8,128)(2,1)S(1)} collective-permute-done((bf16[768,384]{1,0:T(8,128)(2,1)S(1)}, bf16[768,384]{1,0:T(8,128)(2,1)S(1)}, u32[]{:S(2)}, u32[]{:S(2)}) %collective-permute-start.11) | collective-permute-done | bytes 589856 | tf_op jit(solution)/shard_map/ppermute | solution.py:423
  20.9 17.2 %conditional.1 = (bf16[192,768]{1,0:T(8,128)(2,1)S(1)}) conditional(s32[]{:T(128)} %bitcast, (s32[16,384]{1,0:T(8,128)S(1)}, bf16[384,384]{1,0:T(8,128)(2,1)S(1)}, bf16[384,384]{1,0:T(8,128)(2,1)S(1)}, bf16[768,384]{1,0:T(8,128)(2,1)S(1)}, f32[392,384]{1,0:T(8,128)S(1)}, /*index=5*/f32[392,384]{1,0:T(8,128)S(1)}, bf16[384,384]{1,0:T(8,128)(2,1)S(1)}, ...), branch_computations={%region_0.0_spmd, %region_1.0_spmd} | conditional | flops 7247757312 | bytes 16761080 | solution.py:468
  20.9 2.0 %attend.9 = bf16[864,384]{1,0:T(8,128)(2,1)S(1)} custom-call(s32[16,384]{1,0:T(8,128)S(1)} %get-tuple-element.52.bounds_ref, bf16[384,384]{1,0:T(8,128)(2,1)S(1)} %get-tuple-element.60.refs_0_, bf16[384,384]{1,0:T(8,128)(2,1)S(1)} %get-tuple-element.61.refs_1_, bf16[768,384]{1,0:T(8,128)(2,1)S(1)} %get-tuple-element.55.refs_2_, ...), custom_call_target="tpu_custom_call" | custom-call | flops 905969664 | bytes 1769472 | tf_op jit(solution)/shard_map/cond/branch_0_fun/attend/pallas_call | solution.py:266
  22.9 0.1 collective-permute-start
  23.0 2.0 %attend.8 = (f32[392,384]{1,0:T(8,128)S(1)}, f32[392,384]{1,0:T(8,128)S(1)}) custom-call(s32[16,384]{1,0:T(8,128)S(1)} %get-tuple-element.52.bounds_ref, bf16[384,384]{1,0:T(8,128)(2,1)S(1)} %get-tuple-element.53.refs_0_, bf16[384,384]{1,0:T(8,128)(2,1)S(1)} %get-tuple-element.54.refs_1_, bf16[768,384]{1,0:T(8,128)(2,1)S(1)} %get-tuple-element.55.refs_2_, ...), custom_call_target="tpu_custom_call" | custom-call | flops 905969664 | bytes 1769472 | tf_op jit(solution)/shard_map/cond/branch_0_fun/attend/pallas_call | solution.py:266
  25.0 0.1 collective-permute-done.refs_2_
  25.1 0.6 %message.2 = (bf16[208,384]{1,0:T(8,128)(2,1)S(1)}, bf16[208,384]{1,0:T(8,128)(2,1)S(1)}, bf16[208,384]{1,0:T(8,128)(2,1)S(1)}, bf16[208,384]{1,0:T(8,128)(2,1)S(1)}) custom-call(f32[392,384]{1,0:T(8,128)S(1)} %get-tuple-element.58.refs_0_, f32[392,384]{1,0:T(8,128)S(1)} %get-tuple-element.59.refs_1_, bf16[864,384]{1,0:T(8,128)(2,1)S(1)} %collective-permute-done.refs_2_), custom_call_target="tpu_custom_call" | custom-call | tf_op jit(solution)/shard_map/cond/branch_0_fun/message/pallas_call | solution.py:351
  25.7 3.3 %collective-permute-start.1 = (bf16[208,384]{1,0:T(8,128)(2,1)S(1)}, bf16[208,384]{1,0:T(8,128)(2,1)S(1)}, u32[]{:S(2)}, u32[]{:S(2)}) collective-permute-start(bf16[208,384]{1,0:T(8,128)(2,1)S(1)} %get-tuple-element.64), channel_id=1, source_target_pairs={{5,0},{4,1},{7,2},{6,3},{1,4},{0,5},{3,6},{2,7},{13,8},{12,9},{15,... | collective-permute-start | bytes 479240 | tf_op jit(solution)/shard_map/cond/branch_0_fun/ppermute | solution.py:454
  28.9 0.0 collective-permute-start.2
  28.9 0.6 %collective-permute-start.3 = (bf16[208,384]{1,0:T(8,128)(2,1)S(1)}, bf16[208,384]{1,0:T(8,128)(2,1)S(1)}, u32[]{:S(2)}, u32[]{:S(2)}) collective-permute-start(bf16[208,384]{1,0:T(8,128)(2,1)S(1)} %get-tuple-element.66), channel_id=1, source_target_pairs={{4,0},{6,2},{0,4},{2,6},{12,8},{14,10},{8,12},{10,14},{20,16},{22,... | collective-permute-start | bytes 479240 | tf_op jit(solution)/shard_map/cond/branch_0_fun/ppermute | solution.py:423
  29.6 4.3 %collective-permute-done.1.refs_0_ = bf16[208,384]{1,0:T(8,128)(2,1)S(1)} collective-permute-done((bf16[208,384]{1,0:T(8,128)(2,1)S(1)}, bf16[208,384]{1,0:T(8,128)(2,1)S(1)}, u32[]{:S(2)}, u32[]{:S(2)}) %collective-permute-start.1) | collective-permute-done | bytes 159776 | tf_op jit(solution)/shard_map/cond/branch_0_fun/ppermute | solution.py:454
  33.9 2.5 %collective-permute-done.2.refs_1_ = bf16[208,384]{1,0:T(8,128)(2,1)S(1)} collective-permute-done((bf16[208,384]{1,0:T(8,128)(2,1)S(1)}, bf16[208,384]{1,0:T(8,128)(2,1)S(1)}, u32[]{:S(2)}, u32[]{:S(2)}) %collective-permute-start.2) | collective-permute-done | bytes 159776 | tf_op jit(solution)/shard_map/cond/branch_0_fun/ppermute | solution.py:456
  36.5 0.6 %collective-permute-done.3.refs_2_ = bf16[208,384]{1,0:T(8,128)(2,1)S(1)} collective-permute-done((bf16[208,384]{1,0:T(8,128)(2,1)S(1)}, bf16[208,384]{1,0:T(8,128)(2,1)S(1)}, u32[]{:S(2)}, u32[]{:S(2)}) %collective-permute-start.3) | collective-permute-done | bytes 159776 | tf_op jit(solution)/shard_map/cond/branch_0_fun/ppermute | solution.py:423
  37.1 0.8 %settle.2 = bf16[192,768]{1,0:T(8,128)(2,1)S(1)} custom-call(bf16[208,384]{1,0:T(8,128)(2,1)S(1)} %collective-permute-done.1.refs_0_, bf16[208,384]{1,0:T(8,128)(2,1)S(1)} %collective-permute-done.2.refs_1_, bf16[208,384]{1,0:T(8,128)(2,1)S(1)} %collective-permute-done.3.refs_2_, bf16[208,384]{1,0:T(8,128)(2,1)S(1)} %get-tuple-element.67.refs_3_), custom_call_target="tpu_custom_call" | custom-call | tf_op jit(solution)/shard_map/cond/branch_0_fun/settle/pallas_call | solution.py:388
  38.1 0.0 copy-start.1
  38.1 0.7 %copy-done.1 = bf16[192,768]{1,0:T(8,128)(2,1)} copy-done((bf16[192,768]{1,0:T(8,128)(2,1)}, bf16[192,768]{1,0:T(8,128)(2,1)S(1)}, u32[]{:S(2)}) %copy-start.1) | copy-done | bytes 294936
Async XLA Ops:
  0.0 7.7 %copy-start.2 = (bf16[384,384]{1,0:T(8,128)(2,1)S(1)}, bf16[384,384]{1,0:T(8,128)(2,1)}, u32[]{:S(2)}) copy-start(bf16[384,384]{1,0:T(8,128)(2,1)} %refs_0_.3) | copy-start | bytes 884740
  0.0 11.6 %copy-start = (s32[5]{0:T(128)S(1)}, s32[5]{0:T(128)}, u32[]{:S(2)}) copy-start(s32[5]{0:T(128)} %tiles_ref.1) | copy-start | bytes 64
  0.0 10.3 %collective-permute-start.10 = (bf16[384,384]{1,0:T(8,128)(2,1)}, bf16[384,384]{1,0:T(8,128)(2,1)S(1)}, u32[]{:S(2)}, u32[]{:S(2)}) collective-permute-start(bf16[384,384]{1,0:T(8,128)(2,1)} %refs_0_.3), channel_id=1, source_target_pairs={{4,0},{6,2},{0,4},{2,6},{12,8},{14,10},{8,12},{10,14},{20,16},{22,... | collective-permute-start | bytes 884744 | tf_op jit(solution)/shard_map/ppermute | solution.py:423
  4.2 14.0 %collective-permute-start.14 = (bf16[768,384]{1,0:T(8,128)(2,1)S(1)}, bf16[768,384]{1,0:T(8,128)(2,1)S(1)}, u32[]{:S(2)}, u32[]{:S(2)}) collective-permute-start(bf16[768,384]{1,0:T(8,128)(2,1)S(1)} %pack.1.refs_2_), channel_id=1, source_target_pairs={{10,2},{12,4},{0,8},{18,10},{20,12},{6,14},{8,16},{26,18},{28,20},... | collective-permute-start | bytes 1769480 | tf_op jit(solution)/shard_map/ppermute | solution.py:423
  7.7 5.7 %collective-permute-start.12 = (bf16[384,384]{1,0:T(8,128)(2,1)S(1)}, bf16[384,384]{1,0:T(8,128)(2,1)S(1)}, u32[]{:S(2)}, u32[]{:S(2)}) collective-permute-start(bf16[384,384]{1,0:T(8,128)(2,1)S(1)} %copy-done.2), channel_id=1, source_target_pairs={{2,0},{0,2},{6,4},{4,6},{10,8},{8,10},{14,12},{12,14},{18,16},{16,... | collective-permute-start | bytes 884744 | tf_op jit(solution)/shard_map/ppermute | solution.py:423
  7.8 13.1 %collective-permute-start.11 = (bf16[768,384]{1,0:T(8,128)(2,1)S(1)}, bf16[768,384]{1,0:T(8,128)(2,1)S(1)}, u32[]{:S(2)}, u32[]{:S(2)}) collective-permute-start(bf16[768,384]{1,0:T(8,128)(2,1)S(1)} %pack.1.refs_2_), channel_id=1, source_target_pairs={{8,0},{14,6},{16,8},{2,10},{4,12},{22,14},{24,16},{10,18},{12,20},... | collective-permute-start | bytes 1769480 | tf_op jit(solution)/shard_map/ppermute | solution.py:423
  10.3 5.2 %collective-permute-start.13 = (bf16[384,384]{1,0:T(8,128)(2,1)S(1)}, bf16[384,384]{1,0:T(8,128)(2,1)S(1)}, u32[]{:S(2)}, u32[]{:S(2)}) collective-permute-start(bf16[384,384]{1,0:T(8,128)(2,1)S(1)} %collective-permute-done.10.refs_0_.refs_2_), channel_id=1, source_target_pairs={{2,0},{0,2},{6,4},{4,6},{10,8},{8,10},{14,12},{12,14},{18,16},{16,... | collective-permute-start | bytes 884744 | tf_op jit(solution)/shard_map/ppermute | solution.py:423
  22.9 2.2 %collective-permute-start = (bf16[864,384]{1,0:T(8,128)(2,1)S(1)}, bf16[864,384]{1,0:T(8,128)(2,1)S(1)}, u32[]{:S(2)}, u32[]{:S(2)}) collective-permute-start(bf16[864,384]{1,0:T(8,128)(2,1)S(1)} %attend.9), channel_id=1, source_target_pairs={{2,0},{0,2},{6,4},{4,6},{10,8},{8,10},{14,12},{12,14},{18,16},{16,... | collective-permute-start | bytes 1990664 | tf_op jit(solution)/shard_map/cond/branch_0_fun/ppermute | solution.py:423
  25.7 8.3 %collective-permute-start.1 = (bf16[208,384]{1,0:T(8,128)(2,1)S(1)}, bf16[208,384]{1,0:T(8,128)(2,1)S(1)}, u32[]{:S(2)}, u32[]{:S(2)}) collective-permute-start(bf16[208,384]{1,0:T(8,128)(2,1)S(1)} %get-tuple-element.64), channel_id=1, source_target_pairs={{5,0},{4,1},{7,2},{6,3},{1,4},{0,5},{3,6},{2,7},{13,8},{12,9},{15,... | collective-permute-start | bytes 479240 | tf_op jit(solution)/shard_map/cond/branch_0_fun/ppermute | solution.py:454
  28.9 7.5 %collective-permute-start.2 = (bf16[208,384]{1,0:T(8,128)(2,1)S(1)}, bf16[208,384]{1,0:T(8,128)(2,1)S(1)}, u32[]{:S(2)}, u32[]{:S(2)}) collective-permute-start(bf16[208,384]{1,0:T(8,128)(2,1)S(1)} %get-tuple-element.65), channel_id=1, source_target_pairs={{0,1},{1,0},{2,3},{3,2},{4,5},{5,4},{6,7},{7,6},{8,9},{9,8},{10,11... | collective-permute-start | bytes 479240 | tf_op jit(solution)/shard_map/cond/branch_0_fun/ppermute | solution.py:456
  28.9 8.1 %collective-permute-start.3 = (bf16[208,384]{1,0:T(8,128)(2,1)S(1)}, bf16[208,384]{1,0:T(8,128)(2,1)S(1)}, u32[]{:S(2)}, u32[]{:S(2)}) collective-permute-start(bf16[208,384]{1,0:T(8,128)(2,1)S(1)} %get-tuple-element.66), channel_id=1, source_target_pairs={{4,0},{6,2},{0,4},{2,6},{12,8},{14,10},{8,12},{10,14},{20,16},{22,... | collective-permute-start | bytes 479240 | tf_op jit(solution)/shard_map/cond/branch_0_fun/ppermute | solution.py:423
  38.1 0.7 %copy-start.1 = (bf16[192,768]{1,0:T(8,128)(2,1)}, bf16[192,768]{1,0:T(8,128)(2,1)S(1)}, u32[]{:S(2)}) copy-start(bf16[192,768]{1,0:T(8,128)(2,1)S(1)} %get-tuple-element.139) | copy-start | bytes 884740

commit v3 on v2

--- a/solution.py
+++ b/solution.py
@@ -165,7 +165,8 @@
             state[half, columns + heads :] = jnp.zeros((state.shape[1] - columns - heads, rows), jnp.float32)
         else:
             state[half] = old_refs[half][...]
-    for slot, (array, shift) in enumerate(arrays):
+    alone = len(arrays) == 1
+    for slot, (array, shift) in enumerate([] if alone else arrays):
         size = array_refs[array].shape[0]
         if size < held.shape[1]:
             held[slot] = jnp.zeros(held.shape[1:], held.dtype)
@@ -178,6 +179,11 @@
 
     def chosen(at, options):
         return functools.reduce(lambda x, i: jnp.where(at == i, options[i], x), range(1, len(options)), options[0])
+
+    def piece(slot, at, h):
+        if alone:
+            return array_refs[0][tile_rows(at), head_columns(h)]
+        return held[slot, tile_rows(at), head_columns(h)]
 
     def fold(half, slot, first):
         row = 2 * (which[0] + half * (which[-1] - which[0]) // max(len(which) - 1, 1))
@@ -191,7 +197,7 @@
         totals = [state[half, pl.ds(columns + heads + h, 1), :] for h in range(heads)]
         scores = [
             lax.dot_general(
-                jnp.concatenate([held[slot, tile_rows(2 * j), head_columns(h)] for j in range(count)], axis=0),
+                jnp.concatenate([piece(slot, 2 * j, h) for j in range(count)], axis=0),
                 held_q[half, :, head_columns(h)],
                 (((1,), (1,)), ((), ())),
                 preferred_element_type=jnp.float32,
@@ -215,7 +221,7 @@
                 rounded.append(jnp.concatenate([w.astype(jnp.bfloat16) for w in weights], axis=0))
             updates.append(
                 jnp.dot(
-                    jnp.concatenate([held[slot, tile_rows(2 * j + 1), head_columns(h)] for j in range(count)], axis=1),
+                    jnp.concatenate([piece(slot, 2 * j + 1, h) for j in range(count)], axis=1),
                     jnp.concatenate(rounded, axis=1),
                     preferred_element_type=jnp.float32,
                 )
@@ -312,51 +318,49 @@
     )(*states)
 
 
-def message_kernel(*refs):
-    states, got_ref, outs, held = refs[:2], refs[2], refs[3:7], refs[7]
-    rows = outs[0].shape[0] - 2 * 8
-    columns = outs[0].shape[1]
+def message_kernel(part, ref, got_ref, *refs):
+    keep_ref, send_ref, held = refs[-3:]
+    rows = keep_ref.shape[0] - 2 * 8
+    columns = keep_ref.shape[1]
     heads = columns // HEAD_DIM
     mine = lax.axis_index("head")
-    for part in range(2):
-        ref, (keep_ref, send_ref) = states[part], outs[2 * part : 2 * part + 2]
-        at = part * got_ref.shape[0] // 2
-        logs = []
-        rest = got_ref[at + columns : at + got_ref.shape[0] // 2].astype(jnp.float32)
-        statistics = functools.reduce(jnp.add, [rest[n * 2 * 8 : n * 2 * 8 + 8] for n in range(3)])
-        for h in range(heads):
-            maxima = [ref[columns + h : columns + h + 1], statistics[h : h + 1]]
-            totals = [ref[columns + heads + h : columns + heads + h + 1], statistics[heads + h : heads + h + 1]]
-            largest = jnp.maximum(*maxima)
-            factors = [jnp.exp2((m - largest) * SCALE2) for m in maxima]
-            total = factors[0] * totals[0] + factors[1] * totals[1]
-            some = jnp.where(total > 0, total, 1.0)
-            scale = [f / some for f in factors]
-            own = head_columns(h)
-            got = got_ref[at + h * HEAD_DIM : at + (h + 1) * HEAD_DIM].astype(jnp.float32)
-            sums = ref[own] * scale[0] + got * scale[1]
-            held[:, own] = sums.T.astype(held.dtype)
-            log = jnp.where(total > 0, largest * SCALE2 + jnp.log2(some), LOWEST)
-            logs += [part.astype(jnp.float32) for part in summands(log)]
-        logs = jnp.concatenate(logs + [jnp.zeros((2 * 8 - len(logs), held.shape[0]), jnp.float32)], axis=0)
-        later = pltpu.roll(logs, rows, 1)
-        for out_ref, which in ((send_ref, 1 - mine), (keep_ref, mine)):
-            out_ref[:rows] = held[pl.ds(pl.multiple_of(which * rows, 2 * 8), rows), :]
-            out_ref[rows:] = jnp.where(which == 0, logs, later).astype(out_ref.dtype)
-
-
-def messages(mine, peer, got):
-    rows, columns = mine.shape[1], mine.shape[0] // HEAD_DIM * HEAD_DIM
+    at = part * got_ref.shape[0] // 2
+    logs = []
+    rest = got_ref[at + columns : at + got_ref.shape[0] // 2].astype(jnp.float32)
+    statistics = functools.reduce(jnp.add, [rest[n * 2 * 8 : n * 2 * 8 + 8] for n in range(3)])
+    for h in range(heads):
+        maxima = [ref[columns + h : columns + h + 1], statistics[h : h + 1]]
+        totals = [ref[columns + heads + h : columns + heads + h + 1], statistics[heads + h : heads + h + 1]]
+        largest = jnp.maximum(*maxima)
+        factors = [jnp.exp2((m - largest) * SCALE2) for m in maxima]
+        total = factors[0] * totals[0] + factors[1] * totals[1]
+        some = jnp.where(total > 0, total, 1.0)
+        scale = [f / some for f in factors]
+        own = head_columns(h)
+        got = got_ref[at + h * HEAD_DIM : at + (h + 1) * HEAD_DIM].astype(jnp.float32)
+        sums = ref[own] * scale[0] + got * scale[1]
+        held[:, own] = sums.T.astype(held.dtype)
+        log = jnp.where(total > 0, largest * SCALE2 + jnp.log2(some), LOWEST)
+        logs += [part.astype(jnp.float32) for part in summands(log)]
+    logs = jnp.concatenate(logs + [jnp.zeros((2 * 8 - len(logs), held.shape[0]), jnp.float32)], axis=0)
+    later = pltpu.roll(logs, rows, 1)
+    for out_ref, which in ((send_ref, 1 - mine), (keep_ref, mine)):
+        out_ref[:rows] = held[pl.ds(pl.multiple_of(which * rows, 2 * 8), rows), :]
+        out_ref[rows:] = jnp.where(which == 0, logs, later).astype(out_ref.dtype)
+
+
+def messages(part, state, got, *after):
+    rows, columns = state.shape[1], state.shape[0] // HEAD_DIM * HEAD_DIM
     shape = jax.ShapeDtypeStruct((rows // 2 + 2 * 8, columns), jnp.bfloat16)
     return pl.pallas_call(
-        message_kernel,
-        out_shape=[shape] * 4,
-        in_specs=[VMEM] * 3,
-        out_specs=[VMEM] * 4,
+        functools.partial(message_kernel, part),
+        out_shape=[shape] * 2,
+        in_specs=[VMEM] * 2 + [HBM] * len(after),
+        out_specs=[VMEM] * 2,
         scratch_shapes=[pltpu.VMEM((rows, columns), jnp.bfloat16)],
         compiler_params=params(),
         name="message",
-    )(mine, peer, got)
+    )(state, got, *after)
 
 
 def settle_kernel(*refs):
@@ -449,7 +453,8 @@
         (others,) = fold(blocks, places, states, which=[1, 3], shifts=shifts, brief=True)
         got = moved(others, sibling)
         mine, peer = fold(blocks, places, states, which=[0, 2], shifts=shifts)
-        keep, over_x, over_y, over_both = messages(mine, peer, got)
+        over_y, over_both = messages(1, peer, got)
+        keep, over_x = messages(0, mine, got, over_y)
         pairs = [(2 * across(s) + 1 - x, 2 * s + x) for s in owners for x in range(2)]
         over_both = lax.ppermute(over_both, ("seq", "head"), pairs)
         over_y = moved(over_y, across)

time: 38.9 us -> 55.5 us (1.43)
  waiting for transfers between devices: 11.5 us -> 27.9 us
  starting transfers between devices: 13.2 us -> 15 us
  Pallas kernels: 12.5 us -> 11.1 us
    ppermute x7 -> x9, waiting for transfers between devices: 4.6 us -> 22.7 us  [moved(): return lax.ppermute(array, 'seq', pairs)]
    ppermute x7 -> x9, starting transfers between devices: 9.89 us -> 13.4 us  [moved(): return lax.ppermute(array, 'seq', pairs)]
    ppermute x1, starting transfers between devices: 3.29 us -> 0.01 us  [merge(): over_both = lax.ppermute(over_both, ('seq', 'head'), pairs)]
    ppermute x1, waiting for transfers between devices: 4.35 us -> 1.76 us  [merge(): over_both = lax.ppermute(over_both, ('seq', 'head'), pairs)]
    ppermute x1, starting transfers between devices: 0.01 us -> 1.55 us  [merge(): over_x = lax.ppermute(over_x, 'head', [(0, 1), (1, 0)])]
    pallas_call x5 -> x6, Pallas kernels: 8.65 us -> 7.13 us  [attend(): pl.pallas_call(functools.partial(attend_kernel, which, places, arrays, no...]
    ppermute x1, waiting for transfers between devices: 2.52 us -> 3.46 us  [merge(): over_x = lax.ppermute(over_x, 'head', [(0, 1), (1, 0)])]
  transfers between devices with their start and end apart: 9 -> 11, of which waited for: 7 -> 8; matrix products, arithmetic and copies ran while one was open for 0% -> 0% of each run, Pallas kernels for 23% -> 15%
where the time goes in v3:
time: 55.5 us; the launch traced here: 55.7 us
  waiting for transfers between devices  27.9 us (50%)
  starting transfers between devices  15 us (27%)
  Pallas kernels  11.1 us (20%)
  between operations  0.76 us (1%)
  local copies, waits for them, and re-layouts  0.72 us (1%)
    ppermute x9, waiting for transfers between devices, moved(): return lax.ppermute(array, 'seq', pairs)  22.7 us
    ppermute x9, starting transfers between devices, moved(): return lax.ppermute(array, 'seq', pairs)  13.4 us
    pallas_call x6, Pallas kernels, attend(): pl.pallas_call(functools.partial(attend_kernel, which, places, arrays, no...  7.13 us
    ppermute x1, waiting for transfers between devices, merge(): over_x = lax.ppermute(over_x, 'head', [(0, 1), (1, 0)])  3.46 us
    ppermute x1, waiting for transfers between devices, merge(): over_both = lax.ppermute(over_both, ('seq', 'head'), pairs)  1.76 us
    ppermute x1, starting transfers between devices, merge(): over_x = lax.ppermute(over_x, 'head', [(0, 1), (1, 0)])  1.55 us
    pallas_call x1, Pallas kernels, pack(): pl.pallas_call(pack_kernel, out_shape=jax.ShapeDtypeStruct((2 * rows, col...  1.22 us
    pallas_call x1, Pallas kernels, meta(): pl.pallas_call(functools.partial(meta_kernel, halves), out_shape=[jax.Sha...  1.22 us
  transfers between devices with their start and end apart: 11, of which 8 were waited for; matrix products, arithmetic and copies ran while one was open for 0% of the time, Pallas kernels for 15%

profile of v3, /device:TPU:0, one launch (start us, length us, event | category | flops | bytes accessed | tf_op | source)
XLA Modules:
  0.0 55.7 jit_solution(7267381340720231580)
XLA Ops:
  0.0 0.0 copy-start.2
  0.0 0.0 copy-start
  0.0 3.0 %collective-permute-start.10 = (bf16[384,384]{1,0:T(8,128)(2,1)}, bf16[384,384]{1,0:T(8,128)(2,1)S(1)}, u32[]{:S(2)}, u32[]{:S(2)}) collective-permute-start(bf16[384,384]{1,0:T(8,128)(2,1)} %refs_0_.3), channel_id=1, source_target_pairs={{4,0},{6,2},{0,4},{2,6},{12,8},{14,10},{8,12},{10,14},{20,16},{22,... | collective-permute-start | bytes 884744 | tf_op jit(solution)/shard_map/ppermute | solution.py:427
  3.0 1.2 %pack.1.refs_2_ = bf16[768,384]{1,0:T(8,128)(2,1)S(1)} custom-call(bf16[384,384]{1,0:T(8,128)(2,1)} %k_ref.1, bf16[384,384]{1,0:T(8,128)(2,1)} %v_ref.1), custom_call_target="tpu_custom_call" | custom-call | tf_op jit(solution)/shard_map/pack/pallas_call | solution.py:100
  4.2 3.5 %collective-permute-start.14 = (bf16[768,384]{1,0:T(8,128)(2,1)S(1)}, bf16[768,384]{1,0:T(8,128)(2,1)S(1)}, u32[]{:S(2)}, u32[]{:S(2)}) collective-permute-start(bf16[768,384]{1,0:T(8,128)(2,1)S(1)} %pack.1.refs_2_), channel_id=1, source_target_pairs={{10,2},{12,4},{0,8},{18,10},{20,12},{6,14},{8,16},{26,18},{28,20},... | collective-permute-start | bytes 1769480 | tf_op jit(solution)/shard_map/ppermute | solution.py:427
  7.7 0.0 copy-done.2
  7.7 0.1 collective-permute-start.12
  7.8 1.3 %collective-permute-start.11 = (bf16[768,384]{1,0:T(8,128)(2,1)S(1)}, bf16[768,384]{1,0:T(8,128)(2,1)S(1)}, u32[]{:S(2)}, u32[]{:S(2)}) collective-permute-start(bf16[768,384]{1,0:T(8,128)(2,1)S(1)} %pack.1.refs_2_), channel_id=1, source_target_pairs={{8,0},{14,6},{16,8},{2,10},{4,12},{22,14},{24,16},{10,18},{12,20},... | collective-permute-start | bytes 1769480 | tf_op jit(solution)/shard_map/ppermute | solution.py:427
  9.1 1.1 %collective-permute-done.10.refs_0_.refs_2_ = bf16[384,384]{1,0:T(8,128)(2,1)S(1)} collective-permute-done((bf16[384,384]{1,0:T(8,128)(2,1)}, bf16[384,384]{1,0:T(8,128)(2,1)S(1)}, u32[]{:S(2)}, u32[]{:S(2)}) %collective-permute-start.10) | collective-permute-done | bytes 294944 | tf_op jit(solution)/shard_map/ppermute | solution.py:427
  10.3 1.3 %collective-permute-start.13 = (bf16[384,384]{1,0:T(8,128)(2,1)S(1)}, bf16[384,384]{1,0:T(8,128)(2,1)S(1)}, u32[]{:S(2)}, u32[]{:S(2)}) collective-permute-start(bf16[384,384]{1,0:T(8,128)(2,1)S(1)} %collective-permute-done.10.refs_0_.refs_2_), channel_id=1, source_target_pairs={{2,0},{0,2},{6,4},{4,6},{10,8},{8,10},{14,12},{12,14},{18,16},{16,... | collective-permute-start | bytes 884744 | tf_op jit(solution)/shard_map/ppermute | solution.py:427
  11.6 0.0 copy-done
  11.6 1.2 %meta.1 = (s32[16,384]{1,0:T(8,128)S(1)}, s32[1]{0:T(128)}) custom-call(s32[5]{0:T(128)S(1)} %copy-done), custom_call_target="tpu_custom_call" | custom-call | flops 536870912 | tf_op jit(solution)/shard_map/meta/pallas_call | solution.py:69
  13.5 0.0 collective-permute-done.12.refs_1_
  13.5 2.0 %attend.13 = (f32[392,384]{1,0:T(8,128)S(1)}, f32[392,384]{1,0:T(8,128)S(1)}) custom-call(s32[16,384]{1,0:T(8,128)S(1)} %get-tuple-element.103.bounds_ref, bf16[384,384]{1,0:T(8,128)(2,1)S(1)} %copy-done.2, bf16[384,384]{1,0:T(8,128)(2,1)S(1)} %collective-permute-done.12.refs_1_, bf16[768,384]{1,0:T(8,128)(2,1)S(1)} %pack.1.refs_2_), custom_call_target="tpu_custom_call" | custom-call | flops 905969664 | bytes 1769472 | tf_op jit(solution)/shard_map/attend/pallas_call | solution.py:272
  15.5 0.0 collective-permute-done.13.refs_1_.refs_3_
  15.5 1.1 %attend.14 = (f32[392,384]{1,0:T(8,128)S(1)}, f32[392,384]{1,0:T(8,128)S(1)}) custom-call(s32[16,384]{1,0:T(8,128)S(1)} %get-tuple-element.103.bounds_ref, bf16[384,384]{1,0:T(8,128)(2,1)S(1)} %collective-permute-done.10.refs_0_.refs_2_, bf16[384,384]{1,0:T(8,128)(2,1)S(1)} %collective-permute-done.13.refs_1_.refs_3_, bf16[768,384]{1,0:T(8,128)(2,1)S(1)} %pack.1.refs_2_), custom_call_target="tpu_custom_call" | custom-call | flops 905969664 | bytes 1769472 | tf_op jit(solution)/shard_map/attend/pallas_call | solution.py:272
  16.6 1.6 %collective-permute-done.14.refs_4_ = bf16[768,384]{1,0:T(8,128)(2,1)S(1)} collective-permute-done((bf16[768,384]{1,0:T(8,128)(2,1)S(1)}, bf16[768,384]{1,0:T(8,128)(2,1)S(1)}, u32[]{:S(2)}, u32[]{:S(2)}) %collective-permute-start.14) | collective-permute-done | bytes 589856 | tf_op jit(solution)/shard_map/ppermute | solution.py:427
  18.2 0.6 %attend.15 = (f32[392,384]{1,0:T(8,128)S(1)}, f32[392,384]{1,0:T(8,128)S(1)}, f32[392,384]{1,0:T(8,128)S(1)}, f32[392,384]{1,0:T(8,128)S(1)}) custom-call(s32[16,384]{1,0:T(8,128)S(1)} %get-tuple-element.103.bounds_ref, bf16[384,384]{1,0:T(8,128)(2,1)S(1)} %copy-done.2, bf16[384,384]{1,0:T(8,128)(2,1)S(1)} %collective-permute-done.12.refs_1_, ...), custom_call_target="tpu_custom_call" | custom-call | flops 1811939328 | bytes 2949120 | tf_op jit(solution)/shard_map/attend/pallas_call | solution.py:272
  18.8 2.1 %collective-permute-done.11 = bf16[768,384]{1,0:T(8,128)(2,1)S(1)} collective-permute-done((bf16[768,384]{1,0:T(8,128)(2,1)S(1)}, bf16[768,384]{1,0:T(8,128)(2,1)S(1)}, u32[]{:S(2)}, u32[]{:S(2)}) %collective-permute-start.11) | collective-permute-done | bytes 589856 | tf_op jit(solution)/shard_map/ppermute | solution.py:427
  20.9 34.1 %conditional.1 = (bf16[192,768]{1,0:T(8,128)(2,1)S(1)}) conditional(s32[]{:T(128)} %bitcast, (s32[16,384]{1,0:T(8,128)S(1)}, bf16[384,384]{1,0:T(8,128)(2,1)S(1)}, bf16[384,384]{1,0:T(8,128)(2,1)S(1)}, bf16[768,384]{1,0:T(8,128)(2,1)S(1)}, f32[392,384]{1,0:T(8,128)S(1)}, /*index=5*/f32[392,384]{1,0:T(8,128)S(1)}, bf16[384,384]{1,0:T(8,128)(2,1)S(1)}, ...), branch_computations={%region_0.0_spmd, %region_1.0_spmd} | conditional | flops 7247757312 | bytes 16761080 | solution.py:473
  20.9 0.1 onward.1
  21.0 1.3 %collective-permute-start.4 = (bf16[768,384]{1,0:T(8,128)(2,1)S(1)}, bf16[768,384]{1,0:T(8,128)(2,1)S(1)}, u32[]{:S(2)}, u32[]{:S(2)}) collective-permute-start(bf16[768,384]{1,0:T(8,128)(2,1)S(1)} %get-tuple-element.74), channel_id=1, source_target_pairs={{8,0},{10,2},{16,8},{18,10},{4,12},{6,14},{24,16},{26,18},{12,20},... | collective-permute-start | bytes 1769480 | tf_op jit(solution)/shard_map/cond/branch_1_fun/ppermute | solution.py:427
  22.3 0.9 %collective-permute-start.5 = (bf16[512,384]{1,0:T(8,128)(2,1)S(1)}, bf16[512,384]{1,0:T(8,128)(2,1)S(1)}, u32[]{:S(2)}, u32[]{:S(2)}) collective-permute-start(bf16[512,384]{1,0:T(8,128)(2,1)S(1)} %get-tuple-element.75), channel_id=1, source_target_pairs={{12,4},{2,10},{20,12},{10,18},{28,20},{18,26},{13,5},{3,11},{21,13... | collective-permute-start | bytes 1179656 | tf_op jit(solution)/shard_map/cond/branch_1_fun/ppermute | solution.py:427
  23.2 1.7 %attend.10 = (f32[392,384]{1,0:T(8,128)S(1)}, f32[392,384]{1,0:T(8,128)S(1)}, f32[392,384]{1,0:T(8,128)S(1)}, f32[392,384]{1,0:T(8,128)S(1)}) custom-call(s32[16,384]{1,0:T(8,128)S(1)} %get-tuple-element.68.bounds_ref, bf16[384,384]{1,0:T(8,128)(2,1)S(1)} %get-tuple-element.69.refs_0_, bf16[384,384]{1,0:T(8,128)(2,1)S(1)} %get-tuple-element.76.refs_1_.refs_0_, ...), custom_call_target="tpu_custom_call" | custom-call | flops 3623878656 | bytes 3538944 | tf_op jit(solution)/shard_map/cond/branch_1_fun/attend/pallas_call | solution.py:272
  24.8 0.0 collective-permute-done.5.refs_3_
  24.8 14.1 %collective-permute-done.4.refs_2_ = bf16[768,384]{1,0:T(8,128)(2,1)S(1)} collective-permute-done((bf16[768,384]{1,0:T(8,128)(2,1)S(1)}, bf16[768,384]{1,0:T(8,128)(2,1)S(1)}, u32[]{:S(2)}, u32[]{:S(2)}) %collective-permute-start.4) | collective-permute-done | bytes 589856 | tf_op jit(solution)/shard_map/cond/branch_1_fun/ppermute | solution.py:427
  39.0 1.3 %attend.12 = bf16[864,384]{1,0:T(8,128)(2,1)S(1)} custom-call(s32[16,384]{1,0:T(8,128)S(1)} %get-tuple-element.68.bounds_ref, bf16[384,384]{1,0:T(8,128)(2,1)S(1)} %get-tuple-element.76.refs_1_.refs_0_, bf16[384,384]{1,0:T(8,128)(2,1)S(1)} %get-tuple-element.77.refs_3_.refs_1_, bf16[768,384]{1,0:T(8,128)(2,1)S(1)} %collective-permute-done.4.refs_2_, ...), custom_call_target="tpu_custom_call" | custom-call | flops 1811939328 | bytes 2359296 | tf_op jit(solution)/shard_map/cond/branch_1_fun/attend/pallas_call | solution.py:272
  40.3 0.1 collective-permute-start.6
  40.4 0.5 attend.11
  40.9 1.6 %collective-permute-done.6.got_ref = bf16[864,384]{1,0:T(8,128)(2,1)S(1)} collective-permute-done((bf16[864,384]{1,0:T(8,128)(2,1)S(1)}, bf16[864,384]{1,0:T(8,128)(2,1)S(1)}, u32[]{:S(2)}, u32[]{:S(2)}) %collective-permute-start.6) | collective-permute-done | bytes 663584 | tf_op jit(solution)/shard_map/cond/branch_1_fun/ppermute | solution.py:427
  42.5 0.3 message.6
  42.8 0.3 message.7
  43.1 1.5 %collective-permute-start.8 = (bf16[208,384]{1,0:T(8,128)(2,1)S(1)}, bf16[208,384]{1,0:T(8,128)(2,1)S(1)}, u32[]{:S(2)}, u32[]{:S(2)}) collective-permute-start(bf16[208,384]{1,0:T(8,128)(2,1)S(1)} %get-tuple-element.90), channel_id=1, source_target_pairs={{0,1},{1,0},{2,3},{3,2},{4,5},{5,4},{6,7},{7,6},{8,9},{9,8},{10,11... | collective-permute-start | bytes 479240 | tf_op jit(solution)/shard_map/cond/branch_1_fun/ppermute | solution.py:461
  44.7 0.0 collective-permute-start.7
  44.7 2.0 %collective-permute-start.9 = (bf16[208,384]{1,0:T(8,128)(2,1)S(1)}, bf16[208,384]{1,0:T(8,128)(2,1)S(1)}, u32[]{:S(2)}, u32[]{:S(2)}) collective-permute-start(bf16[208,384]{1,0:T(8,128)(2,1)S(1)} %get-tuple-element.89.refs_0_), channel_id=1, source_target_pairs={{4,0},{6,2},{0,4},{2,6},{12,8},{14,10},{8,12},{10,14},{20,16},{22,... | collective-permute-start | bytes 479240 | tf_op jit(solution)/shard_map/cond/branch_1_fun/ppermute | solution.py:427
  46.7 3.5 %collective-permute-done.8.refs_1_ = bf16[208,384]{1,0:T(8,128)(2,1)S(1)} collective-permute-done((bf16[208,384]{1,0:T(8,128)(2,1)S(1)}, bf16[208,384]{1,0:T(8,128)(2,1)S(1)}, u32[]{:S(2)}, u32[]{:S(2)}) %collective-permute-start.8) | collective-permute-done | bytes 159776 | tf_op jit(solution)/shard_map/cond/branch_1_fun/ppermute | solution.py:461
  50.1 1.8 %collective-permute-done.7.refs_0_ = bf16[208,384]{1,0:T(8,128)(2,1)S(1)} collective-permute-done((bf16[208,384]{1,0:T(8,128)(2,1)S(1)}, bf16[208,384]{1,0:T(8,128)(2,1)S(1)}, u32[]{:S(2)}, u32[]{:S(2)}) %collective-permute-start.7) | collective-permute-done | bytes 159776 | tf_op jit(solution)/shard_map/cond/branch_1_fun/ppermute | solution.py:459
  51.9 2.1 %collective-permute-done.9.refs_2_ = bf16[208,384]{1,0:T(8,128)(2,1)S(1)} collective-permute-done((bf16[208,384]{1,0:T(8,128)(2,1)S(1)}, bf16[208,384]{1,0:T(8,128)(2,1)S(1)}, u32[]{:S(2)}, u32[]{:S(2)}) %collective-permute-start.9) | collective-permute-done | bytes 159776 | tf_op jit(solution)/shard_map/cond/branch_1_fun/ppermute | solution.py:427
  54.0 0.8 %settle.3 = bf16[192,768]{1,0:T(8,128)(2,1)S(1)} custom-call(bf16[208,384]{1,0:T(8,128)(2,1)S(1)} %collective-permute-done.7.refs_0_, bf16[208,384]{1,0:T(8,128)(2,1)S(1)} %collective-permute-done.8.refs_1_, bf16[208,384]{1,0:T(8,128)(2,1)S(1)} %collective-permute-done.9.refs_2_, bf16[208,384]{1,0:T(8,128)(2,1)S(1)} %get-tuple-element.91.refs_3_), custom_call_target="tpu_custom_call" | custom-call | tf_op jit(solution)/shard_map/cond/branch_1_fun/settle/pallas_call | solution.py:392
  55.0 0.0 copy-start.1
  55.0 0.7 %copy-done.1 = bf16[192,768]{1,0:T(8,128)(2,1)} copy-done((bf16[192,768]{1,0:T(8,128)(2,1)}, bf16[192,768]{1,0:T(8,128)(2,1)S(1)}, u32[]{:S(2)}) %copy-start.1) | copy-done | bytes 294936
Async XLA Ops:
  0.0 7.7 %copy-start.2 = (bf16[384,384]{1,0:T(8,128)(2,1)S(1)}, bf16[384,384]{1,0:T(8,128)(2,1)}, u32[]{:S(2)}) copy-start(bf16[384,384]{1,0:T(8,128)(2,1)} %refs_0_.3) | copy-start | bytes 884740
  0.0 11.6 %copy-start = (s32[5]{0:T(128)S(1)}, s32[5]{0:T(128)}, u32[]{:S(2)}) copy-start(s32[5]{0:T(128)} %tiles_ref.1) | copy-start | bytes 64
  0.0 10.3 %collective-permute-start.10 = (bf16[384,384]{1,0:T(8,128)(2,1)}, bf16[384,384]{1,0:T(8,128)(2,1)S(1)}, u32[]{:S(2)}, u32[]{:S(2)}) collective-permute-start(bf16[384,384]{1,0:T(8,128)(2,1)} %refs_0_.3), channel_id=1, source_target_pairs={{4,0},{6,2},{0,4},{2,6},{12,8},{14,10},{8,12},{10,14},{20,16},{22,... | collective-permute-start | bytes 884744 | tf_op jit(solution)/shard_map/ppermute | solution.py:427
  4.2 14.0 %collective-permute-start.14 = (bf16[768,384]{1,0:T(8,128)(2,1)S(1)}, bf16[768,384]{1,0:T(8,128)(2,1)S(1)}, u32[]{:S(2)}, u32[]{:S(2)}) collective-permute-start(bf16[768,384]{1,0:T(8,128)(2,1)S(1)} %pack.1.refs_2_), channel_id=1, source_target_pairs={{10,2},{12,4},{0,8},{18,10},{20,12},{6,14},{8,16},{26,18},{28,20},... | collective-permute-start | bytes 1769480 | tf_op jit(solution)/shard_map/ppermute | solution.py:427
  7.7 5.7 %collective-permute-start.12 = (bf16[384,384]{1,0:T(8,128)(2,1)S(1)}, bf16[384,384]{1,0:T(8,128)(2,1)S(1)}, u32[]{:S(2)}, u32[]{:S(2)}) collective-permute-start(bf16[384,384]{1,0:T(8,128)(2,1)S(1)} %copy-done.2), channel_id=1, source_target_pairs={{2,0},{0,2},{6,4},{4,6},{10,8},{8,10},{14,12},{12,14},{18,16},{16,... | collective-permute-start | bytes 884744 | tf_op jit(solution)/shard_map/ppermute | solution.py:427
  7.8 13.1 %collective-permute-start.11 = (bf16[768,384]{1,0:T(8,128)(2,1)S(1)}, bf16[768,384]{1,0:T(8,128)(2,1)S(1)}, u32[]{:S(2)}, u32[]{:S(2)}) collective-permute-start(bf16[768,384]{1,0:T(8,128)(2,1)S(1)} %pack.1.refs_2_), channel_id=1, source_target_pairs={{8,0},{14,6},{16,8},{2,10},{4,12},{22,14},{24,16},{10,18},{12,20},... | collective-permute-start | bytes 1769480 | tf_op jit(solution)/shard_map/ppermute | solution.py:427
  10.3 5.2 %collective-permute-start.13 = (bf16[384,384]{1,0:T(8,128)(2,1)S(1)}, bf16[384,384]{1,0:T(8,128)(2,1)S(1)}, u32[]{:S(2)}, u32[]{:S(2)}) collective-permute-start(bf16[384,384]{1,0:T(8,128)(2,1)S(1)} %collective-permute-done.10.refs_0_.refs_2_), channel_id=1, source_target_pairs={{2,0},{0,2},{6,4},{4,6},{10,8},{8,10},{14,12},{12,14},{18,16},{16,... | collective-permute-start | bytes 884744 | tf_op jit(solution)/shard_map/ppermute | solution.py:427
  21.0 18.0 %collective-permute-start.4 = (bf16[768,384]{1,0:T(8,128)(2,1)S(1)}, bf16[768,384]{1,0:T(8,128)(2,1)S(1)}, u32[]{:S(2)}, u32[]{:S(2)}) collective-permute-start(bf16[768,384]{1,0:T(8,128)(2,1)S(1)} %get-tuple-element.74), channel_id=1, source_target_pairs={{8,0},{10,2},{16,8},{18,10},{4,12},{6,14},{24,16},{26,18},{12,20},... | collective-permute-start | bytes 1769480 | tf_op jit(solution)/shard_map/cond/branch_1_fun/ppermute | solution.py:427
  22.3 2.5 %collective-permute-start.5 = (bf16[512,384]{1,0:T(8,128)(2,1)S(1)}, bf16[512,384]{1,0:T(8,128)(2,1)S(1)}, u32[]{:S(2)}, u32[]{:S(2)}) collective-permute-start(bf16[512,384]{1,0:T(8,128)(2,1)S(1)} %get-tuple-element.75), channel_id=1, source_target_pairs={{12,4},{2,10},{20,12},{10,18},{28,20},{18,26},{13,5},{3,11},{21,13... | collective-permute-start | bytes 1179656 | tf_op jit(solution)/shard_map/cond/branch_1_fun/ppermute | solution.py:427
  40.3 2.2 %collective-permute-start.6 = (bf16[864,384]{1,0:T(8,128)(2,1)S(1)}, bf16[864,384]{1,0:T(8,128)(2,1)S(1)}, u32[]{:S(2)}, u32[]{:S(2)}) collective-permute-start(bf16[864,384]{1,0:T(8,128)(2,1)S(1)} %attend.12), channel_id=1, source_target_pairs={{2,0},{0,2},{6,4},{4,6},{10,8},{8,10},{14,12},{12,14},{18,16},{16,... | collective-permute-start | bytes 1990664 | tf_op jit(solution)/shard_map/cond/branch_1_fun/ppermute | solution.py:427
  43.1 7.0 %collective-permute-start.8 = (bf16[208,384]{1,0:T(8,128)(2,1)S(1)}, bf16[208,384]{1,0:T(8,128)(2,1)S(1)}, u32[]{:S(2)}, u32[]{:S(2)}) collective-permute-start(bf16[208,384]{1,0:T(8,128)(2,1)S(1)} %get-tuple-element.90), channel_id=1, source_target_pairs={{0,1},{1,0},{2,3},{3,2},{4,5},{5,4},{6,7},{7,6},{8,9},{9,8},{10,11... | collective-permute-start | bytes 479240 | tf_op jit(solution)/shard_map/cond/branch_1_fun/ppermute | solution.py:461
  44.7 7.2 %collective-permute-start.7 = (bf16[208,384]{1,0:T(8,128)(2,1)S(1)}, bf16[208,384]{1,0:T(8,128)(2,1)S(1)}, u32[]{:S(2)}, u32[]{:S(2)}) collective-permute-start(bf16[208,384]{1,0:T(8,128)(2,1)S(1)} %get-tuple-element.87), channel_id=1, source_target_pairs={{5,0},{4,1},{7,2},{6,3},{1,4},{0,5},{3,6},{2,7},{13,8},{12,9},{15,... | collective-permute-start | bytes 479240 | tf_op jit(solution)/shard_map/cond/branch_1_fun/ppermute | solution.py:459
  44.7 9.3 %collective-permute-start.9 = (bf16[208,384]{1,0:T(8,128)(2,1)S(1)}, bf16[208,384]{1,0:T(8,128)(2,1)S(1)}, u32[]{:S(2)}, u32[]{:S(2)}) collective-permute-start(bf16[208,384]{1,0:T(8,128)(2,1)S(1)} %get-tuple-element.89.refs_0_), channel_id=1, source_target_pairs={{4,0},{6,2},{0,4},{2,6},{12,8},{14,10},{8,12},{10,14},{20,16},{22,... | collective-permute-start | bytes 479240 | tf_op jit(solution)/shard_map/cond/branch_1_fun/ppermute | solution.py:427
  55.0 0.7 %copy-start.1 = (bf16[192,768]{1,0:T(8,128)(2,1)}, bf16[192,768]{1,0:T(8,128)(2,1)S(1)}, u32[]{:S(2)}) copy-start(bf16[192,768]{1,0:T(8,128)(2,1)S(1)} %get-tuple-element.139) | copy-start | bytes 884740

commit v4 on v3

--- a/solution.py
+++ b/solution.py
@@ -364,7 +364,7 @@
 
 
 def settle_kernel(*refs):
-    parts, out_ref, logs = refs[:4], refs[4], refs[5]
+    parts, out_ref, logs = [refs[0], refs[2], refs[1], refs[3]], refs[4], refs[5]
     rows, columns = out_ref.shape[0], parts[0].shape[1]
     heads = columns // HEAD_DIM
     mine = lax.axis_index("head")
@@ -387,7 +387,7 @@
             out_ref[:, pl.ds(at, HEAD_DIM)] = done.astype(out_ref.dtype)
 
 
-def settle(diagonal, beside, across, own):
+def settle(diagonal, across, beside, own):
     rows, columns = own.shape[0] - 2 * 8, own.shape[1]
     return pl.pallas_call(
         settle_kernel,
@@ -397,7 +397,7 @@
         scratch_shapes=[pltpu.VMEM((TILE, columns), jnp.float32)],
         compiler_params=params(),
         name="settle",
-    )(diagonal, beside, across, own)
+    )(diagonal, across, beside, own)
 
 
 def chip_pairs(mesh):
@@ -459,7 +459,7 @@
         over_both = lax.ppermute(over_both, ("seq", "head"), pairs)
         over_y = moved(over_y, across)
         over_x = lax.ppermute(over_x, "head", [(0, 1), (1, 0)])
-        return settle(over_both, over_x, over_y, keep)
+        return settle(over_both, over_y, over_x, keep)
 
     def near_only(block, a1, b1, states):
         return merge([a1], [A1], states)

time: 55.5 us -> 55.2 us (level)
  waiting for transfers between devices: 27.9 us -> 26.9 us
    ppermute x9, waiting for transfers between devices: 22.7 us -> 21.5 us  [moved(): return lax.ppermute(array, 'seq', pairs)]
  transfers between devices with their start and end apart: 11 -> 11, of which waited for: 8 -> 8; matrix products, arithmetic and copies ran while one was open for 0% -> 0% of each run, Pallas kernels for 15% -> 17%
where the time goes in v4:
time: 55.2 us; the launch traced here: 54.9 us
  waiting for transfers between devices  26.9 us (49%)
  starting transfers between devices  15.1 us (27%)
  Pallas kernels  11.1 us (20%)
  between operations  0.76 us (1%)
  local copies, waits for them, and re-layouts  0.72 us (1%)
    ppermute x9, waiting for transfers between devices, moved(): return lax.ppermute(array, 'seq', pairs)  21.5 us
    ppermute x9, starting transfers between devices, moved(): return lax.ppermute(array, 'seq', pairs)  13.5 us
    pallas_call x6, Pallas kernels, attend(): pl.pallas_call(functools.partial(attend_kernel, which, places, arrays, no...  7.14 us
    ppermute x1, waiting for transfers between devices, merge(): over_x = lax.ppermute(over_x, 'head', [(0, 1), (1, 0)])  3.46 us
    ppermute x1, waiting for transfers between devices, merge(): over_both = lax.ppermute(over_both, ('seq', 'head'), pairs)  1.93 us
    ppermute x1, starting transfers between devices, merge(): over_x = lax.ppermute(over_x, 'head', [(0, 1), (1, 0)])  1.55 us
    pallas_call x1, Pallas kernels, pack(): pl.pallas_call(pack_kernel, out_shape=jax.ShapeDtypeStruct((2 * rows, col...  1.22 us
    pallas_call x1, Pallas kernels, meta(): pl.pallas_call(functools.partial(meta_kernel, halves), out_shape=[jax.Sha...  1.22 us
  transfers between devices with their start and end apart: 11, of which 8 were waited for; matrix products, arithmetic and copies ran while one was open for 0% of the time, Pallas kernels for 17%

profile of v4, /device:TPU:0, one launch (start us, length us, event | category | flops | bytes accessed | tf_op | source)
XLA Modules:
  0.0 54.9 jit_solution(2735908466675779478)
XLA Ops:
  0.0 0.0 copy-start.2
  0.0 0.0 copy-start
  0.0 3.0 %collective-permute-start.10 = (bf16[384,384]{1,0:T(8,128)(2,1)}, bf16[384,384]{1,0:T(8,128)(2,1)S(1)}, u32[]{:S(2)}, u32[]{:S(2)}) collective-permute-start(bf16[384,384]{1,0:T(8,128)(2,1)} %refs_0_.3), channel_id=1, source_target_pairs={{4,0},{6,2},{0,4},{2,6},{12,8},{14,10},{8,12},{10,14},{20,16},{22,... | collective-permute-start | bytes 884744 | tf_op jit(solution)/shard_map/ppermute | solution.py:427
  3.0 1.2 %pack.1.refs_2_ = bf16[768,384]{1,0:T(8,128)(2,1)S(1)} custom-call(bf16[384,384]{1,0:T(8,128)(2,1)} %k_ref.1, bf16[384,384]{1,0:T(8,128)(2,1)} %v_ref.1), custom_call_target="tpu_custom_call" | custom-call | tf_op jit(solution)/shard_map/pack/pallas_call | solution.py:100
  4.2 3.5 %collective-permute-start.14 = (bf16[768,384]{1,0:T(8,128)(2,1)S(1)}, bf16[768,384]{1,0:T(8,128)(2,1)S(1)}, u32[]{:S(2)}, u32[]{:S(2)}) collective-permute-start(bf16[768,384]{1,0:T(8,128)(2,1)S(1)} %pack.1.refs_2_), channel_id=1, source_target_pairs={{10,2},{12,4},{0,8},{18,10},{20,12},{6,14},{8,16},{26,18},{28,20},... | collective-permute-start | bytes 1769480 | tf_op jit(solution)/shard_map/ppermute | solution.py:427
  7.7 0.0 copy-done.2
  7.7 0.1 collective-permute-start.12
  7.8 1.3 %collective-permute-start.11 = (bf16[768,384]{1,0:T(8,128)(2,1)S(1)}, bf16[768,384]{1,0:T(8,128)(2,1)S(1)}, u32[]{:S(2)}, u32[]{:S(2)}) collective-permute-start(bf16[768,384]{1,0:T(8,128)(2,1)S(1)} %pack.1.refs_2_), channel_id=1, source_target_pairs={{8,0},{14,6},{16,8},{2,10},{4,12},{22,14},{24,16},{10,18},{12,20},... | collective-permute-start | bytes 1769480 | tf_op jit(solution)/shard_map/ppermute | solution.py:427
  9.1 1.1 %collective-permute-done.10.refs_0_.refs_2_ = bf16[384,384]{1,0:T(8,128)(2,1)S(1)} collective-permute-done((bf16[384,384]{1,0:T(8,128)(2,1)}, bf16[384,384]{1,0:T(8,128)(2,1)S(1)}, u32[]{:S(2)}, u32[]{:S(2)}) %collective-permute-start.10) | collective-permute-done | bytes 294944 | tf_op jit(solution)/shard_map/ppermute | solution.py:427
  10.3 1.3 %collective-permute-start.13 = (bf16[384,384]{1,0:T(8,128)(2,1)S(1)}, bf16[384,384]{1,0:T(8,128)(2,1)S(1)}, u32[]{:S(2)}, u32[]{:S(2)}) collective-permute-start(bf16[384,384]{1,0:T(8,128)(2,1)S(1)} %collective-permute-done.10.refs_0_.refs_2_), channel_id=1, source_target_pairs={{2,0},{0,2},{6,4},{4,6},{10,8},{8,10},{14,12},{12,14},{18,16},{16,... | collective-permute-start | bytes 884744 | tf_op jit(solution)/shard_map/ppermute | solution.py:427
  11.6 0.0 copy-done
  11.6 1.2 %meta.1 = (s32[16,384]{1,0:T(8,128)S(1)}, s32[1]{0:T(128)}) custom-call(s32[5]{0:T(128)S(1)} %copy-done), custom_call_target="tpu_custom_call" | custom-call | flops 536870912 | tf_op jit(solution)/shard_map/meta/pallas_call | solution.py:69
  13.5 0.0 collective-permute-done.12.refs_1_
  13.5 2.0 %attend.13 = (f32[392,384]{1,0:T(8,128)S(1)}, f32[392,384]{1,0:T(8,128)S(1)}) custom-call(s32[16,384]{1,0:T(8,128)S(1)} %get-tuple-element.103.bounds_ref, bf16[384,384]{1,0:T(8,128)(2,1)S(1)} %copy-done.2, bf16[384,384]{1,0:T(8,128)(2,1)S(1)} %collective-permute-done.12.refs_1_, bf16[768,384]{1,0:T(8,128)(2,1)S(1)} %pack.1.refs_2_), custom_call_target="tpu_custom_call" | custom-call | flops 905969664 | bytes 1769472 | tf_op jit(solution)/shard_map/attend/pallas_call | solution.py:272
  15.5 0.0 collective-permute-done.13.refs_1_.refs_3_
  15.5 2.0 %attend.14 = (f32[392,384]{1,0:T(8,128)S(1)}, f32[392,384]{1,0:T(8,128)S(1)}) custom-call(s32[16,384]{1,0:T(8,128)S(1)} %get-tuple-element.103.bounds_ref, bf16[384,384]{1,0:T(8,128)(2,1)S(1)} %collective-permute-done.10.refs_0_.refs_2_, bf16[384,384]{1,0:T(8,128)(2,1)S(1)} %collective-permute-done.13.refs_1_.refs_3_, bf16[768,384]{1,0:T(8,128)(2,1)S(1)} %pack.1.refs_2_), custom_call_target="tpu_custom_call" | custom-call | flops 905969664 | bytes 1769472 | tf_op jit(solution)/shard_map/attend/pallas_call | solution.py:272
  17.5 0.8 %collective-permute-done.14.refs_4_ = bf16[768,384]{1,0:T(8,128)(2,1)S(1)} collective-permute-done((bf16[768,384]{1,0:T(8,128)(2,1)S(1)}, bf16[768,384]{1,0:T(8,128)(2,1)S(1)}, u32[]{:S(2)}, u32[]{:S(2)}) %collective-permute-start.14) | collective-permute-done | bytes 589856 | tf_op jit(solution)/shard_map/ppermute | solution.py:427
  18.2 0.6 %attend.15 = (f32[392,384]{1,0:T(8,128)S(1)}, f32[392,384]{1,0:T(8,128)S(1)}, f32[392,384]{1,0:T(8,128)S(1)}, f32[392,384]{1,0:T(8,128)S(1)}) custom-call(s32[16,384]{1,0:T(8,128)S(1)} %get-tuple-element.103.bounds_ref, bf16[384,384]{1,0:T(8,128)(2,1)S(1)} %copy-done.2, bf16[384,384]{1,0:T(8,128)(2,1)S(1)} %collective-permute-done.12.refs_1_, ...), custom_call_target="tpu_custom_call" | custom-call | flops 1811939328 | bytes 2949120 | tf_op jit(solution)/shard_map/attend/pallas_call | solution.py:272
  18.8 2.1 %collective-permute-done.11 = bf16[768,384]{1,0:T(8,128)(2,1)S(1)} collective-permute-done((bf16[768,384]{1,0:T(8,128)(2,1)S(1)}, bf16[768,384]{1,0:T(8,128)(2,1)S(1)}, u32[]{:S(2)}, u32[]{:S(2)}) %collective-permute-start.11) | collective-permute-done | bytes 589856 | tf_op jit(solution)/shard_map/ppermute | solution.py:427
  20.9 33.3 %conditional.1 = (bf16[192,768]{1,0:T(8,128)(2,1)S(1)}) conditional(s32[]{:T(128)} %bitcast, (s32[16,384]{1,0:T(8,128)S(1)}, bf16[384,384]{1,0:T(8,128)(2,1)S(1)}, bf16[384,384]{1,0:T(8,128)(2,1)S(1)}, bf16[768,384]{1,0:T(8,128)(2,1)S(1)}, f32[392,384]{1,0:T(8,128)S(1)}, /*index=5*/f32[392,384]{1,0:T(8,128)S(1)}, bf16[384,384]{1,0:T(8,128)(2,1)S(1)}, ...), branch_computations={%region_0.0_spmd, %region_1.0_spmd} | conditional | flops 7247757312 | bytes 16761080 | solution.py:473
  20.9 0.1 onward.1
  21.0 1.3 %collective-permute-start.4 = (bf16[768,384]{1,0:T(8,128)(2,1)S(1)}, bf16[768,384]{1,0:T(8,128)(2,1)S(1)}, u32[]{:S(2)}, u32[]{:S(2)}) collective-permute-start(bf16[768,384]{1,0:T(8,128)(2,1)S(1)} %get-tuple-element.74), channel_id=1, source_target_pairs={{8,0},{10,2},{16,8},{18,10},{4,12},{6,14},{24,16},{26,18},{12,20},... | collective-permute-start | bytes 1769480 | tf_op jit(solution)/shard_map/cond/branch_1_fun/ppermute | solution.py:427
  22.3 0.9 %collective-permute-start.5 = (bf16[512,384]{1,0:T(8,128)(2,1)S(1)}, bf16[512,384]{1,0:T(8,128)(2,1)S(1)}, u32[]{:S(2)}, u32[]{:S(2)}) collective-permute-start(bf16[512,384]{1,0:T(8,128)(2,1)S(1)} %get-tuple-element.75), channel_id=1, source_target_pairs={{12,4},{2,10},{20,12},{10,18},{28,20},{18,26},{13,5},{3,11},{21,13... | collective-permute-start | bytes 1179656 | tf_op jit(solution)/shard_map/cond/branch_1_fun/ppermute | solution.py:427
  23.2 1.7 %attend.10 = (f32[392,384]{1,0:T(8,128)S(1)}, f32[392,384]{1,0:T(8,128)S(1)}, f32[392,384]{1,0:T(8,128)S(1)}, f32[392,384]{1,0:T(8,128)S(1)}) custom-call(s32[16,384]{1,0:T(8,128)S(1)} %get-tuple-element.68.bounds_ref, bf16[384,384]{1,0:T(8,128)(2,1)S(1)} %get-tuple-element.69.refs_0_, bf16[384,384]{1,0:T(8,128)(2,1)S(1)} %get-tuple-element.76.refs_1_.refs_0_, ...), custom_call_target="tpu_custom_call" | custom-call | flops 3623878656 | bytes 3538944 | tf_op jit(solution)/shard_map/cond/branch_1_fun/attend/pallas_call | solution.py:272
  24.8 0.0 collective-permute-done.5.refs_3_
  24.8 14.1 %collective-permute-done.4.refs_2_ = bf16[768,384]{1,0:T(8,128)(2,1)S(1)} collective-permute-done((bf16[768,384]{1,0:T(8,128)(2,1)S(1)}, bf16[768,384]{1,0:T(8,128)(2,1)S(1)}, u32[]{:S(2)}, u32[]{:S(2)}) %collective-permute-start.4) | collective-permute-done | bytes 589856 | tf_op jit(solution)/shard_map/cond/branch_1_fun/ppermute | solution.py:427
  39.0 0.5 attend.12
  39.5 0.2 collective-permute-start.6
  39.6 0.5 attend.11
  40.1 1.5 %collective-permute-done.6.got_ref = bf16[864,384]{1,0:T(8,128)(2,1)S(1)} collective-permute-done((bf16[864,384]{1,0:T(8,128)(2,1)S(1)}, bf16[864,384]{1,0:T(8,128)(2,1)S(1)}, u32[]{:S(2)}, u32[]{:S(2)}) %collective-permute-start.6) | collective-permute-done | bytes 663584 | tf_op jit(solution)/shard_map/cond/branch_1_fun/ppermute | solution.py:427
  41.6 0.3 message.6
  42.0 0.3 message.7
  42.3 1.5 %collective-permute-start.9 = (bf16[208,384]{1,0:T(8,128)(2,1)S(1)}, bf16[208,384]{1,0:T(8,128)(2,1)S(1)}, u32[]{:S(2)}, u32[]{:S(2)}) collective-permute-start(bf16[208,384]{1,0:T(8,128)(2,1)S(1)} %get-tuple-element.90), channel_id=1, source_target_pairs={{0,1},{1,0},{2,3},{3,2},{4,5},{5,4},{6,7},{7,6},{8,9},{9,8},{10,11... | collective-permute-start | bytes 479240 | tf_op jit(solution)/shard_map/cond/branch_1_fun/ppermute | solution.py:461
  43.8 0.0 collective-permute-start.7
  43.8 2.0 %collective-permute-start.8 = (bf16[208,384]{1,0:T(8,128)(2,1)S(1)}, bf16[208,384]{1,0:T(8,128)(2,1)S(1)}, u32[]{:S(2)}, u32[]{:S(2)}) collective-permute-start(bf16[208,384]{1,0:T(8,128)(2,1)S(1)} %get-tuple-element.88.refs_0_), channel_id=1, source_target_pairs={{4,0},{6,2},{0,4},{2,6},{12,8},{14,10},{8,12},{10,14},{20,16},{22,... | collective-permute-start | bytes 479240 | tf_op jit(solution)/shard_map/cond/branch_1_fun/ppermute | solution.py:427
  45.8 3.5 %collective-permute-done.9.refs_2_ = bf16[208,384]{1,0:T(8,128)(2,1)S(1)} collective-permute-done((bf16[208,384]{1,0:T(8,128)(2,1)S(1)}, bf16[208,384]{1,0:T(8,128)(2,1)S(1)}, u32[]{:S(2)}, u32[]{:S(2)}) %collective-permute-start.9) | collective-permute-done | bytes 159776 | tf_op jit(solution)/shard_map/cond/branch_1_fun/ppermute | solution.py:461
  49.3 1.9 %collective-permute-done.7.refs_0_ = bf16[208,384]{1,0:T(8,128)(2,1)S(1)} collective-permute-done((bf16[208,384]{1,0:T(8,128)(2,1)S(1)}, bf16[208,384]{1,0:T(8,128)(2,1)S(1)}, u32[]{:S(2)}, u32[]{:S(2)}) %collective-permute-start.7) | collective-permute-done | bytes 159776 | tf_op jit(solution)/shard_map/cond/branch_1_fun/ppermute | solution.py:459
  51.2 1.9 %collective-permute-done.8.refs_1_ = bf16[208,384]{1,0:T(8,128)(2,1)S(1)} collective-permute-done((bf16[208,384]{1,0:T(8,128)(2,1)S(1)}, bf16[208,384]{1,0:T(8,128)(2,1)S(1)}, u32[]{:S(2)}, u32[]{:S(2)}) %collective-permute-start.8) | collective-permute-done | bytes 159776 | tf_op jit(solution)/shard_map/cond/branch_1_fun/ppermute | solution.py:427
  53.1 0.8 %settle.3 = bf16[192,768]{1,0:T(8,128)(2,1)S(1)} custom-call(bf16[208,384]{1,0:T(8,128)(2,1)S(1)} %collective-permute-done.7.refs_0_, bf16[208,384]{1,0:T(8,128)(2,1)S(1)} %collective-permute-done.8.refs_1_, bf16[208,384]{1,0:T(8,128)(2,1)S(1)} %collective-permute-done.9.refs_2_, bf16[208,384]{1,0:T(8,128)(2,1)S(1)} %get-tuple-element.91.refs_3_), custom_call_target="tpu_custom_call" | custom-call | tf_op jit(solution)/shard_map/cond/branch_1_fun/settle/pallas_call | solution.py:392
  54.2 0.0 copy-start.1
  54.2 0.7 %copy-done.1 = bf16[192,768]{1,0:T(8,128)(2,1)} copy-done((bf16[192,768]{1,0:T(8,128)(2,1)}, bf16[192,768]{1,0:T(8,128)(2,1)S(1)}, u32[]{:S(2)}) %copy-start.1) | copy-done | bytes 294936
Async XLA Ops:
  0.0 7.7 %copy-start.2 = (bf16[384,384]{1,0:T(8,128)(2,1)S(1)}, bf16[384,384]{1,0:T(8,128)(2,1)}, u32[]{:S(2)}) copy-start(bf16[384,384]{1,0:T(8,128)(2,1)} %refs_0_.3) | copy-start | bytes 884740
  0.0 11.6 %copy-start = (s32[5]{0:T(128)S(1)}, s32[5]{0:T(128)}, u32[]{:S(2)}) copy-start(s32[5]{0:T(128)} %tiles_ref.1) | copy-start | bytes 64
  0.0 10.3 %collective-permute-start.10 = (bf16[384,384]{1,0:T(8,128)(2,1)}, bf16[384,384]{1,0:T(8,128)(2,1)S(1)}, u32[]{:S(2)}, u32[]{:S(2)}) collective-permute-start(bf16[384,384]{1,0:T(8,128)(2,1)} %refs_0_.3), channel_id=1, source_target_pairs={{4,0},{6,2},{0,4},{2,6},{12,8},{14,10},{8,12},{10,14},{20,16},{22,... | collective-permute-start | bytes 884744 | tf_op jit(solution)/shard_map/ppermute | solution.py:427
  4.2 14.0 %collective-permute-start.14 = (bf16[768,384]{1,0:T(8,128)(2,1)S(1)}, bf16[768,384]{1,0:T(8,128)(2,1)S(1)}, u32[]{:S(2)}, u32[]{:S(2)}) collective-permute-start(bf16[768,384]{1,0:T(8,128)(2,1)S(1)} %pack.1.refs_2_), channel_id=1, source_target_pairs={{10,2},{12,4},{0,8},{18,10},{20,12},{6,14},{8,16},{26,18},{28,20},... | collective-permute-start | bytes 1769480 | tf_op jit(solution)/shard_map/ppermute | solution.py:427
  7.7 5.7 %collective-permute-start.12 = (bf16[384,384]{1,0:T(8,128)(2,1)S(1)}, bf16[384,384]{1,0:T(8,128)(2,1)S(1)}, u32[]{:S(2)}, u32[]{:S(2)}) collective-permute-start(bf16[384,384]{1,0:T(8,128)(2,1)S(1)} %copy-done.2), channel_id=1, source_target_pairs={{2,0},{0,2},{6,4},{4,6},{10,8},{8,10},{14,12},{12,14},{18,16},{16,... | collective-permute-start | bytes 884744 | tf_op jit(solution)/shard_map/ppermute | solution.py:427
  7.8 13.1 %collective-permute-start.11 = (bf16[768,384]{1,0:T(8,128)(2,1)S(1)}, bf16[768,384]{1,0:T(8,128)(2,1)S(1)}, u32[]{:S(2)}, u32[]{:S(2)}) collective-permute-start(bf16[768,384]{1,0:T(8,128)(2,1)S(1)} %pack.1.refs_2_), channel_id=1, source_target_pairs={{8,0},{14,6},{16,8},{2,10},{4,12},{22,14},{24,16},{10,18},{12,20},... | collective-permute-start | bytes 1769480 | tf_op jit(solution)/shard_map/ppermute | solution.py:427
  10.3 5.2 %collective-permute-start.13 = (bf16[384,384]{1,0:T(8,128)(2,1)S(1)}, bf16[384,384]{1,0:T(8,128)(2,1)S(1)}, u32[]{:S(2)}, u32[]{:S(2)}) collective-permute-start(bf16[384,384]{1,0:T(8,128)(2,1)S(1)} %collective-permute-done.10.refs_0_.refs_2_), channel_id=1, source_target_pairs={{2,0},{0,2},{6,4},{4,6},{10,8},{8,10},{14,12},{12,14},{18,16},{16,... | collective-permute-start | bytes 884744 | tf_op jit(solution)/shard_map/ppermute | solution.py:427
  21.0 18.0 %collective-permute-start.4 = (bf16[768,384]{1,0:T(8,128)(2,1)S(1)}, bf16[768,384]{1,0:T(8,128)(2,1)S(1)}, u32[]{:S(2)}, u32[]{:S(2)}) collective-permute-start(bf16[768,384]{1,0:T(8,128)(2,1)S(1)} %get-tuple-element.74), channel_id=1, source_target_pairs={{8,0},{10,2},{16,8},{18,10},{4,12},{6,14},{24,16},{26,18},{12,20},... | collective-permute-start | bytes 1769480 | tf_op jit(solution)/shard_map/cond/branch_1_fun/ppermute | solution.py:427
  22.3 2.5 %collective-permute-start.5 = (bf16[512,384]{1,0:T(8,128)(2,1)S(1)}, bf16[512,384]{1,0:T(8,128)(2,1)S(1)}, u32[]{:S(2)}, u32[]{:S(2)}) collective-permute-start(bf16[512,384]{1,0:T(8,128)(2,1)S(1)} %get-tuple-element.75), channel_id=1, source_target_pairs={{12,4},{2,10},{20,12},{10,18},{28,20},{18,26},{13,5},{3,11},{21,13... | collective-permute-start | bytes 1179656 | tf_op jit(solution)/shard_map/cond/branch_1_fun/ppermute | solution.py:427
  39.5 2.2 %collective-permute-start.6 = (bf16[864,384]{1,0:T(8,128)(2,1)S(1)}, bf16[864,384]{1,0:T(8,128)(2,1)S(1)}, u32[]{:S(2)}, u32[]{:S(2)}) collective-permute-start(bf16[864,384]{1,0:T(8,128)(2,1)S(1)} %attend.12), channel_id=1, source_target_pairs={{2,0},{0,2},{6,4},{4,6},{10,8},{8,10},{14,12},{12,14},{18,16},{16,... | collective-permute-start | bytes 1990664 | tf_op jit(solution)/shard_map/cond/branch_1_fun/ppermute | solution.py:427
  42.3 7.0 %collective-permute-start.9 = (bf16[208,384]{1,0:T(8,128)(2,1)S(1)}, bf16[208,384]{1,0:T(8,128)(2,1)S(1)}, u32[]{:S(2)}, u32[]{:S(2)}) collective-permute-start(bf16[208,384]{1,0:T(8,128)(2,1)S(1)} %get-tuple-element.90), channel_id=1, source_target_pairs={{0,1},{1,0},{2,3},{3,2},{4,5},{5,4},{6,7},{7,6},{8,9},{9,8},{10,11... | collective-permute-start | bytes 479240 | tf_op jit(solution)/shard_map/cond/branch_1_fun/ppermute | solution.py:461
  43.8 7.4 %collective-permute-start.7 = (bf16[208,384]{1,0:T(8,128)(2,1)S(1)}, bf16[208,384]{1,0:T(8,128)(2,1)S(1)}, u32[]{:S(2)}, u32[]{:S(2)}) collective-permute-start(bf16[208,384]{1,0:T(8,128)(2,1)S(1)} %get-tuple-element.87), channel_id=1, source_target_pairs={{5,0},{4,1},{7,2},{6,3},{1,4},{0,5},{3,6},{2,7},{13,8},{12,9},{15,... | collective-permute-start | bytes 479240 | tf_op jit(solution)/shard_map/cond/branch_1_fun/ppermute | solution.py:459
  43.8 9.3 %collective-permute-start.8 = (bf16[208,384]{1,0:T(8,128)(2,1)S(1)}, bf16[208,384]{1,0:T(8,128)(2,1)S(1)}, u32[]{:S(2)}, u32[]{:S(2)}) collective-permute-start(bf16[208,384]{1,0:T(8,128)(2,1)S(1)} %get-tuple-element.88.refs_0_), channel_id=1, source_target_pairs={{4,0},{6,2},{0,4},{2,6},{12,8},{14,10},{8,12},{10,14},{20,16},{22,... | collective-permute-start | bytes 479240 | tf_op jit(solution)/shard_map/cond/branch_1_fun/ppermute | solution.py:427
  54.2 0.7 %copy-start.1 = (bf16[192,768]{1,0:T(8,128)(2,1)}, bf16[192,768]{1,0:T(8,128)(2,1)S(1)}, u32[]{:S(2)}) copy-start(bf16[192,768]{1,0:T(8,128)(2,1)S(1)} %get-tuple-element.139) | copy-start | bytes 884740
